TPU v7x, 32 devices: a whole 2x2x4 slice. The times are simulated.
32 devices in a mesh: frame: 8 (over y, x, core), tensor: 4 (over z).
Axes of the slice: x: 2, y: 2, z: 4, core: 2. Of those that a mesh axis runs over, the one named last changes fastest.
Arguments:
- latents: bfloat16 [4096, 5120], P('frame', 'tensor'), may hold values from -6 to 6
- w_query: bfloat16 [5120, 3072], P(None, 'tensor'), may hold values from -0.078125 to 0.078125
- w_key: bfloat16 [5120, 3072], P(None, 'tensor'), may hold values from -0.078125 to 0.078125
- w_value: bfloat16 [5120, 3072], P(None, 'tensor'), may hold values from -0.078125 to 0.078125
- w_out: bfloat16 [3072, 5120], P('tensor'), may hold values from -0.109375 to 0.109375
- query_gain: float32 [24, 128], P('tensor'), may hold values from 0.5 to 14, as said below
- key_gain: float32 [24, 128], P('tensor'), may hold values from 0.5 to 14, as said below
- mod_table: float32 [16, 3, 5120], replicated, may hold values from -3 to 3
- levels: int32 [8], P('frame'), may hold values from 0 to 15
- span_counts: int32 [8], replicated, may hold values from 1 to 512, 3072 in all
- block_mask: int32 [8, 8], P('frame'), may hold values 0 or 1
- span_order: int32 [8], replicated, may hold values from 0 to 7, each once
Outputs:
- updated: bfloat16 [4096, 5120], P('frame', 'tensor')
Inputs may be any that keep to these rules, and one draw needn't show every extreme that they name: `query_gain`: gains are positive. `key_gain`: gains are positive. `span_order`: each rank appears once.
All inputs are finite; a program needn't handle non-finite values. No bound on the sum of `block_mask` on one device may be relied on, other than what follows from the above.
Results may differ from a plain program's by a relative error of at most 0.012.
The roundings to bfloat16 on the way count: a program that leaves them out, or rounds other values in their place, can miss the bound.
Values may be sent and summed in bfloat16 or wider, within the bound.
A program may use at most 128 MiB of HBM per device.

v0:
```python
import math

import jax
import jax.numpy as jnp
from jax import lax
from jax.sharding import PartitionSpec as P

HEAD_DIM = 128


EPSILON = 1e-06
NEG_FILL = -1e30


def shifted(block, axis, distance):
    devices = range(lax.axis_size(axis))
    route = [((i - distance) % len(devices), i) for i in devices]
    return lax.ppermute(block, axis, route)


def on_device(
    latents,
    w_query,
    w_key,
    w_value,
    w_out,
    query_gain,
    key_gain,
    mod_table,
    levels,
    span_counts,
    block_mask,
    span_order,
):
    row_count = latents.shape[0]
    shard_width = latents.shape[1]
    span_total = lax.axis_size("frame")
    my_span = lax.axis_index("frame")
    column_start = lax.axis_index("tensor") * shard_width
    selector = jnp.arange(mod_table.shape[0], dtype=jnp.int32) == levels[0]
    modulation = jnp.sum(jnp.where(selector[:, None, None], mod_table, 0.0), axis=0)
    shift_row = modulation[0]
    scale_row = modulation[1]
    gate_row = modulation[2]
    whole = lax.all_gather(latents, "tensor", axis=1, tiled=True).astype(jnp.float32)
    row_mean = jnp.mean(whole, axis=1, keepdims=True)
    row_square = jnp.mean(whole * whole, axis=1, keepdims=True)
    normed = (
        (whole - row_mean)
        * lax.rsqrt(row_square - row_mean * row_mean + EPSILON)
        * (1.0 + scale_row)
        + shift_row
    ).astype(jnp.bfloat16)
    head_local = w_query.shape[1] // HEAD_DIM

    def project(weight, gain_table):
        shaped = jnp.dot(normed, weight, preferred_element_type=jnp.float32).reshape(
            row_count, head_local, HEAD_DIM
        )
        scaled = (
            shaped
            * lax.rsqrt(jnp.mean(shaped * shaped, axis=-1, keepdims=True) + EPSILON)
            * gain_table
        )
        return scaled.astype(jnp.bfloat16)

    queries = project(w_query, query_gain)
    keys_local = project(w_key, key_gain).reshape(row_count, head_local * HEAD_DIM)
    values_local = jnp.dot(normed, w_value, preferred_element_type=jnp.float32).astype(jnp.bfloat16)
    kv_pair = jnp.stack((keys_local, values_local))
    span_ids = jnp.arange(span_total, dtype=jnp.int32)
    my_rank = jnp.sum(jnp.where(span_ids == my_span, span_order, 0))
    mask_row = block_mask[0]
    slot_index = jnp.arange(row_count, dtype=jnp.int32)
    score_factor = 1.0 / math.sqrt(HEAD_DIM)

    def attend(carried, piece, start):
        block_count = piece.shape[1] // row_count
        key_blocks = piece[0].reshape(block_count, row_count, head_local, HEAD_DIM)
        value_blocks = piece[1].reshape(block_count, row_count, head_local, HEAD_DIM)

        def fold_block(running, block):
            key_block, value_block, block_index = block
            source = start // row_count + block_index
            source_count = jnp.sum(jnp.where(span_ids == source, span_counts, 0))
            linked = jnp.sum(jnp.where(span_ids == source, mask_row, 0)) == 1
            source_rank = jnp.sum(jnp.where(span_ids == source, span_order, 0))
            allowed = (source_rank <= my_rank) & (linked | (source == my_span))
            valid = allowed & (slot_index < source_count)
            running_max, running_sum, accum = running
            scores = (
                jnp.einsum("qhd,khd->hqk", queries, key_block, preferred_element_type=jnp.float32)
                * score_factor
            )
            scores = jnp.where(valid[None, None, :], scores, NEG_FILL)
            new_max = jnp.maximum(running_max, jnp.max(scores, axis=-1))
            weights = jnp.where(valid[None, None, :], jnp.exp(scores - new_max[:, :, None]), 0.0)
            factor = jnp.exp(running_max - new_max)
            new_sum = running_sum * factor + jnp.sum(weights, axis=-1)
            new_accum = accum * factor[:, :, None] + jnp.einsum(
                "hqk,khd->hqd",
                weights.astype(jnp.bfloat16),
                value_block,
                preferred_element_type=jnp.float32,
            )
            return ((new_max, new_sum, new_accum), None)

        blocks = (key_blocks, value_blocks, jnp.arange(block_count, dtype=jnp.int32))
        result, unused = lax.scan(fold_block, carried, blocks)
        return result

    initial = (
        jnp.full((head_local, row_count), NEG_FILL, jnp.float32),
        jnp.zeros((head_local, row_count), jnp.float32),
        jnp.zeros((head_local, row_count, HEAD_DIM), jnp.float32),
    )
    carried = attend(initial, kv_pair, my_span * row_count)

    def hand_over(step_index, loop_state):
        running, travelling = loop_state
        travelling = shifted(travelling, "frame", 1)
        source = (my_span - step_index) % span_total
        return (attend(running, travelling, source * row_count), travelling)

    carried, unused_pair = lax.fori_loop(1, span_total, hand_over, (carried, kv_pair))
    running_max, running_sum, accum = carried
    attended = (accum / running_sum[:, :, None]).astype(jnp.bfloat16)
    attended = jnp.transpose(attended, (1, 0, 2)).reshape(row_count, head_local * HEAD_DIM)
    partial_out = jnp.dot(attended, w_out, preferred_element_type=jnp.float32)
    projected = lax.psum_scatter(
        partial_out.astype(jnp.bfloat16), "tensor", scatter_dimension=1, tiled=True
    ).astype(jnp.float32)
    gate_part = lax.dynamic_slice_in_dim(gate_row, column_start, shard_width)
    return (latents.astype(jnp.float32) + gate_part * projected).astype(jnp.bfloat16)


def solution(mesh):
    return jax.shard_map(
        on_device,
        mesh=mesh,
        in_specs=(
            P("frame", "tensor"),
            P(None, "tensor"),
            P(None, "tensor"),
            P(None, "tensor"),
            P("tensor", None),
            P("tensor", None),
            P("tensor", None),
            P(),
            P("frame"),
            P(),
            P("frame", None),
            P(),
        ),
        out_specs=P("frame", "tensor"),
        check_vma=False,
    )
```

profile of v0, /device:TPU:0, one launch (start us, length us, event | category | flops | bytes accessed | tf_op | source)
XLA Modules:
  0.0 477.8 jit_solution(11597217929076706797)
XLA Ops:
  14.7 95.0 %all-gather.2.cloned.1.call-done = bf16[512,5120]{1,0:T(8,128)(2,1)} async-done(((bf16[512,1280]{1,0:T(8,128)(2,1)}), bf16[512,5120]{1,0:T(8,128)(2,1)}) %all-gather.2.cloned.1.call-update) | async-done | bytes 5242896 | tf_op jit(solution)/shard_map/all_gather | solution.py:45
  109.7 4.2 convert_reduce_fusion
  114.0 3.0 fusion.25
  117.0 2.3 copy-done.1
  119.3 4.2 convolution_convert_fusion.1
  124.8 10.4 %fusion.49 = f32[512,768]{1,0:T(8,128)} fusion(bf16[512,5120]{1,0:T(8,128)(2,1)} %copy-done.1, bf16[5120,768]{1,0:T(8,128)(2,1)} %param.16), kind=kOutput, calls=%fused_computation.79 | convolution fusion | flops 4026531840 | bytes 14680064 | tf_op jit(solution)/shard_map/dot_general | solution.py:57
  135.2 6.8 %fusion.48 = f32[512,768]{0,1:T(8,128)S(1)} fusion(bf16[512,5120]{1,0:T(8,128)(2,1)S(1)} %bitcast.50, bf16[5120,768]{1,0:T(8,128)(2,1)} %param.15), kind=kOutput, calls=%fused_computation.78 | convolution fusion | flops 4026531840 | bytes 14680064 | tf_op jit(solution)/shard_map/dot_general | solution.py:57
  142.8 1.9 copy.23
  146.3 3.0 copy.29
  149.3 2.1 fusion.37
  151.4 2.4 pad_maximum_fusion
  153.8 2.6 copy.30
  156.4 2.1 fusion.27
  158.5 1.7 fusion.29
  160.3 3.5 fusion.33
  163.8 201.7 %while.42 = (s32[]{:T(128)}, f32[6,512]{1,0:T(8,128)S(1)}, f32[6,512]{1,0:T(8,128)S(1)}, f32[6,512,128]{2,1,0:T(8,128)}, bf16[2,512,768]{1,2,0:T(8,128)(2,1)}, /...) while((s32[]{:T(128)}, f32[6,512]{1,0:T(8,128)S(1)}, ...), condition=%wide.region_17.18_spmd.clone, body=%wide.region_11.17_spmd.clone.sunk | while | flops 826547328 | bytes 49744576 | solution.py:125
  167.9 17.1 %collective-permute-done = bf16[2,512,768]{1,2,0:T(8,128)(2,1)S(1)} collective-permute-done((bf16[2,512,768]{1,2,0:T(8,128)(2,1)}, bf16[2,512,768]{1,2,0:T(8,128)(2,1)S(1)}, u32[]{:S(2)}, u32[]{:S(2)}) %collective-permute-start) | collective-permute-done | bytes 1572896 | tf_op jit(solution)/shard_map/while/body/eval_jaxpr/ppermute | solution.py:18
  185.1 1.6 fusion.81
  186.8 1.7 fusion.82
  188.5 2.6 multiply_add_fusion.5
  196.6 17.2 %collective-permute-done = bf16[2,512,768]{1,2,0:T(8,128)(2,1)S(1)} collective-permute-done((bf16[2,512,768]{1,2,0:T(8,128)(2,1)}, bf16[2,512,768]{1,2,0:T(8,128)(2,1)S(1)}, u32[]{:S(2)}, u32[]{:S(2)}) %collective-permute-start) | collective-permute-done | bytes 1572896 | tf_op jit(solution)/shard_map/while/body/eval_jaxpr/ppermute | solution.py:18
  213.9 1.6 fusion.81
  215.6 1.7 fusion.82
  217.3 2.6 multiply_add_fusion.5
  225.4 17.2 %collective-permute-done = bf16[2,512,768]{1,2,0:T(8,128)(2,1)S(1)} collective-permute-done((bf16[2,512,768]{1,2,0:T(8,128)(2,1)}, bf16[2,512,768]{1,2,0:T(8,128)(2,1)S(1)}, u32[]{:S(2)}, u32[]{:S(2)}) %collective-permute-start) | collective-permute-done | bytes 1572896 | tf_op jit(solution)/shard_map/while/body/eval_jaxpr/ppermute | solution.py:18
  242.7 1.6 fusion.81
  244.3 1.7 fusion.82
  246.1 2.6 multiply_add_fusion.5
  254.1 17.2 %collective-permute-done = bf16[2,512,768]{1,2,0:T(8,128)(2,1)S(1)} collective-permute-done((bf16[2,512,768]{1,2,0:T(8,128)(2,1)}, bf16[2,512,768]{1,2,0:T(8,128)(2,1)S(1)}, u32[]{:S(2)}, u32[]{:S(2)}) %collective-permute-start) | collective-permute-done | bytes 1572896 | tf_op jit(solution)/shard_map/while/body/eval_jaxpr/ppermute | solution.py:18
  271.5 1.6 fusion.81
  273.1 1.7 fusion.82
  274.8 2.6 multiply_add_fusion.5
  282.9 17.2 %collective-permute-done = bf16[2,512,768]{1,2,0:T(8,128)(2,1)S(1)} collective-permute-done((bf16[2,512,768]{1,2,0:T(8,128)(2,1)}, bf16[2,512,768]{1,2,0:T(8,128)(2,1)S(1)}, u32[]{:S(2)}, u32[]{:S(2)}) %collective-permute-start) | collective-permute-done | bytes 1572896 | tf_op jit(solution)/shard_map/while/body/eval_jaxpr/ppermute | solution.py:18
  300.2 1.6 fusion.81
  301.9 1.7 fusion.82
  303.6 2.6 multiply_add_fusion.5
  311.7 17.2 %collective-permute-done = bf16[2,512,768]{1,2,0:T(8,128)(2,1)S(1)} collective-permute-done((bf16[2,512,768]{1,2,0:T(8,128)(2,1)}, bf16[2,512,768]{1,2,0:T(8,128)(2,1)S(1)}, u32[]{:S(2)}, u32[]{:S(2)}) %collective-permute-start) | collective-permute-done | bytes 1572896 | tf_op jit(solution)/shard_map/while/body/eval_jaxpr/ppermute | solution.py:18
  329.0 1.6 fusion.81
  330.7 1.7 fusion.82
  332.4 2.6 multiply_add_fusion.5
  340.5 17.2 %collective-permute-done = bf16[2,512,768]{1,2,0:T(8,128)(2,1)S(1)} collective-permute-done((bf16[2,512,768]{1,2,0:T(8,128)(2,1)}, bf16[2,512,768]{1,2,0:T(8,128)(2,1)S(1)}, u32[]{:S(2)}, u32[]{:S(2)}) %collective-permute-start) | collective-permute-done | bytes 1572896 | tf_op jit(solution)/shard_map/while/body/eval_jaxpr/ppermute | solution.py:18
  357.8 1.6 fusion.81
  359.4 1.7 fusion.82
  361.2 2.6 multiply_add_fusion.5
  365.5 1.9 copy.32
  367.6 9.3 %convolution_convert_fusion = bf16[512,5120]{1,0:T(8,128)(2,1)} fusion(bf16[512,768]{0,1:T(8,128)(2,1)S(1)} %bitcast.53, bf16[768,5120]{1,0:T(8,128)(2,1)} %param.18), kind=kOutput, calls=%fused_computation.32 | convolution fusion | flops 4029153280 | bytes 13893632 | tf_op jit(solution)/shard_map/dot_general | solution.py:129
  376.9 91.3 %reduce-scatter.2.cloned.1.call-done = bf16[512,1280]{1,0:T(8,128)(2,1)} async-done(((bf16[512,5120]{1,0:T(8,128)(2,1)}), bf16[512,1280]{1,0:T(8,128)(2,1)}) %reduce-scatter.2.cloned.1.call-update) | async-done | bytes 1310736 | tf_op jit(solution)/shard_map/reduce_scatter | solution.py:130
  468.2 2.8 add_convert_fusion
  (140 shorter events, 35.5 us)
Async XLA Ops:
  6.5 103.2 %all-gather.2.cloned.1.call-start = ((), (), s32[]{:S(2)}) async-start(), calls=%async_computation.1 | async-start | bytes 6553600 | tf_op jit(solution)/shard_map/all_gather | solution.py:45
  7.3 461.0 %reduce-scatter.2.cloned.1.call-start = ((), (), s32[]{:S(2)}) async-start(), calls=%async_computation.2 | async-start | bytes 6553600 | tf_op jit(solution)/shard_map/reduce_scatter | solution.py:130
  109.7 4.2 copy-start
  114.0 5.4 %copy-start.12 = (bf16[5120,768]{1,0:T(8,128)(2,1)S(1)}, bf16[5120,768]{1,0:T(8,128)(2,1)}, u32[]{:S(2)}) copy-start(bf16[5120,768]{1,0:T(8,128)(2,1)} %param.17) | copy-start | bytes 23592964
  117.0 2.3 copy-start.1
  123.6 11.5 %copy-start.3 = (bf16[512,768]{1,0:T(8,128)(2,1)}, bf16[512,768]{1,0:T(8,128)(2,1)S(1)}, u32[]{:S(2)}) copy-start(bf16[512,768]{1,0:T(8,128)(2,1)S(1)} %convolution_convert_fusion.1) | copy-start | bytes 2359300
  123.6 11.5 %slice-start = ((s8[5242880]{0:T(1024)(128)(4,1)}), s8[1048576]{0:T(1024)(128)(4,1)S(1)}, s32[]{:S(2)}) async-start(s8[5242880]{0:T(1024)(128)(4,1)} %bitcast.49), calls=%async_computation.3 | async-start | bytes 2097152
  124.8 10.4 %slice-start.1 = ((s8[5242880]{0:T(1024)(128)(4,1)}), s8[4194304]{0:T(1024)(128)(4,1)S(1)}, s32[]{:S(2)}) async-start(s8[5242880]{0:T(1024)(128)(4,1)} %bitcast.49), calls=%async_computation.4 | async-start | bytes 8388608
  135.1 7.1 %copy-start.10 = (f32[6,128]{1,0:T(8,128)S(1)}, f32[6,128]{1,0:T(8,128)}, u32[]{:S(2)}) copy-start(f32[6,128]{1,0:T(8,128)} %param.19) | copy-start | bytes 9220
  142.4 6.9 %copy-start.8 = (f32[6,128]{1,0:T(8,128)S(1)}, f32[6,128]{1,0:T(8,128)}, u32[]{:S(2)}) copy-start(f32[6,128]{1,0:T(8,128)} %param.20) | copy-start | bytes 9220
  158.5 1.7 copy-start.6
  160.3 3.5 copy-start.7
  160.3 3.5 copy-start.9
  160.3 3.5 copy-start.11
  164.0 21.0 %collective-permute-start = (bf16[2,512,768]{1,2,0:T(8,128)(2,1)}, bf16[2,512,768]{1,2,0:T(8,128)(2,1)S(1)}, u32[]{:S(2)}, u32[]{:S(2)}) collective-permute-start(bf16[2,512,768]{1,2,0:T(8,128)(2,1)} %get-tuple-element.625), channel_id=1, source_target_pairs={{28,0},{0,4},{4,8},{8,12},{12,16},{16,20},{20,24},{24,28},{29,1},{... | collective-permute-start | bytes 4718600 | tf_op jit(solution)/shard_map/while/body/eval_jaxpr/ppermute | solution.py:18
  185.1 3.4 copy-start.4
  191.1 1.7 copy-start.5
  192.8 21.0 %collective-permute-start = (bf16[2,512,768]{1,2,0:T(8,128)(2,1)}, bf16[2,512,768]{1,2,0:T(8,128)(2,1)S(1)}, u32[]{:S(2)}, u32[]{:S(2)}) collective-permute-start(bf16[2,512,768]{1,2,0:T(8,128)(2,1)} %get-tuple-element.625), channel_id=1, source_target_pairs={{28,0},{0,4},{4,8},{8,12},{12,16},{16,20},{20,24},{24,28},{29,1},{... | collective-permute-start | bytes 4718600 | tf_op jit(solution)/shard_map/while/body/eval_jaxpr/ppermute | solution.py:18
  213.9 3.4 copy-start.4
  219.9 1.7 copy-start.5
  221.6 21.0 %collective-permute-start = (bf16[2,512,768]{1,2,0:T(8,128)(2,1)}, bf16[2,512,768]{1,2,0:T(8,128)(2,1)S(1)}, u32[]{:S(2)}, u32[]{:S(2)}) collective-permute-start(bf16[2,512,768]{1,2,0:T(8,128)(2,1)} %get-tuple-element.625), channel_id=1, source_target_pairs={{28,0},{0,4},{4,8},{8,12},{12,16},{16,20},{20,24},{24,28},{29,1},{... | collective-permute-start | bytes 4718600 | tf_op jit(solution)/shard_map/while/body/eval_jaxpr/ppermute | solution.py:18
  242.7 3.4 copy-start.4
  248.7 1.7 copy-start.5
  250.4 21.0 %collective-permute-start = (bf16[2,512,768]{1,2,0:T(8,128)(2,1)}, bf16[2,512,768]{1,2,0:T(8,128)(2,1)S(1)}, u32[]{:S(2)}, u32[]{:S(2)}) collective-permute-start(bf16[2,512,768]{1,2,0:T(8,128)(2,1)} %get-tuple-element.625), channel_id=1, source_target_pairs={{28,0},{0,4},{4,8},{8,12},{12,16},{16,20},{20,24},{24,28},{29,1},{... | collective-permute-start | bytes 4718600 | tf_op jit(solution)/shard_map/while/body/eval_jaxpr/ppermute | solution.py:18
  271.4 3.4 copy-start.4
  277.5 1.7 copy-start.5
  279.2 21.0 %collective-permute-start = (bf16[2,512,768]{1,2,0:T(8,128)(2,1)}, bf16[2,512,768]{1,2,0:T(8,128)(2,1)S(1)}, u32[]{:S(2)}, u32[]{:S(2)}) collective-permute-start(bf16[2,512,768]{1,2,0:T(8,128)(2,1)} %get-tuple-element.625), channel_id=1, source_target_pairs={{28,0},{0,4},{4,8},{8,12},{12,16},{16,20},{20,24},{24,28},{29,1},{... | collective-permute-start | bytes 4718600 | tf_op jit(solution)/shard_map/while/body/eval_jaxpr/ppermute | solution.py:18
  300.2 3.4 copy-start.4
  306.2 1.7 copy-start.5
  307.9 21.0 %collective-permute-start = (bf16[2,512,768]{1,2,0:T(8,128)(2,1)}, bf16[2,512,768]{1,2,0:T(8,128)(2,1)S(1)}, u32[]{:S(2)}, u32[]{:S(2)}) collective-permute-start(bf16[2,512,768]{1,2,0:T(8,128)(2,1)} %get-tuple-element.625), channel_id=1, source_target_pairs={{28,0},{0,4},{4,8},{8,12},{12,16},{16,20},{20,24},{24,28},{29,1},{... | collective-permute-start | bytes 4718600 | tf_op jit(solution)/shard_map/while/body/eval_jaxpr/ppermute | solution.py:18
  329.0 3.4 copy-start.4
  335.0 1.7 copy-start.5
  336.7 21.0 %collective-permute-start = (bf16[2,512,768]{1,2,0:T(8,128)(2,1)}, bf16[2,512,768]{1,2,0:T(8,128)(2,1)S(1)}, u32[]{:S(2)}, u32[]{:S(2)}) collective-permute-start(bf16[2,512,768]{1,2,0:T(8,128)(2,1)} %get-tuple-element.625), channel_id=1, source_target_pairs={{28,0},{0,4},{4,8},{8,12},{12,16},{16,20},{20,24},{24,28},{29,1},{... | collective-permute-start | bytes 4718600 | tf_op jit(solution)/shard_map/while/body/eval_jaxpr/ppermute | solution.py:18
  357.8 3.4 copy-start.4
  363.8 1.7 copy-start.5
  376.9 91.4 %copy-start.2 = (bf16[512,1280]{1,0:T(8,128)(2,1)S(1)}, bf16[512,1280]{1,0:T(8,128)(2,1)}, u32[]{:S(2)}) copy-start(bf16[512,1280]{1,0:T(8,128)(2,1)} %param.14) | copy-start | bytes 3932164
Sparse Core Ops, SparseCore 0:
  8.9 100.7 all-gather.1
  377.0 91.1 reduce-scatter.1
where the time goes:
time: 479 us; the launch traced here: 478 us
  waiting for transfers between devices  307 us (64%)
  matrix products  66.1 us (14%)
  other arithmetic  47.1 us (10%)
  local copies, waits for them, and re-layouts  27.2 us (6%)
  between operations  16.3 us (3%)
  loops' own time  13.6 us (3%)
    ppermute x7, waiting for transfers between devices, shifted(): return lax.ppermute(block, axis, route)  120 us
    all_gather x1, waiting for transfers between devices, on_device(): lax.all_gather(latents, 'tensor', axis=1, tiled=True).astype(jnp.float32)  95 us
    reduce_scatter x1, waiting for transfers between devices, on_device(): lax.psum_scatter(partial_out.astype(jnp.bfloat16), 'tensor', scatter_dime...  91.3 us
    dot_general x8, matrix products, fold_block(): jnp.einsum('hqk,khd->hqd', weights.astype(jnp.bfloat16), value_block, pre...  21.9 us
    dot_general x2, matrix products, project(): jnp.dot(normed, weight, preferred_element_type=jnp.float32)  17.2 us
    another operation x1, loops' own time, on_device(): lax.fori_loop(1, span_total, hand_over, (carried, kv_pair))  13.6 us
    dot_general x8, matrix products, fold_block(): jnp.einsum('qhd,khd->hqk', queries, key_block, preferred_element_type=jnp...  13.6 us
    reduce_sum x8, other arithmetic, fold_block(): new_sum = running_sum * factor + jnp.sum(weights, axis=-1)  13.4 us
  transfers between devices with their start and end apart: 9, of which 9 were waited for; matrix products, arithmetic and copies ran while one was open for 4% of the time, Pallas kernels for 0%

commit v1 on v0

v1 whole, which is shorter than its diff:
```python
import functools
import math

import jax
import jax.numpy as jnp
from jax import lax
from jax.experimental import pallas as pl
from jax.experimental.pallas import tpu as pltpu
from jax.sharding import PartitionSpec as P

HEAD_DIM = 128
EPSILON = 1e-06
NEG_FILL = -1e30
GATHER_PARTS = 4
QUERY_PARTS = 2
VMEM_BYTES = 56 * 1024 * 1024
FACTOR = math.log2(math.e) / math.sqrt(HEAD_DIM)


def qkv_kernel(x_ref, shift_ref, scale_ref, wq_ref, wk_ref, wv_ref, qg_ref, kg_ref, q_ref, kv_ref, normed_ref):
    shards, rows, width = x_ref.shape
    heads = q_ref.shape[0]

    @pl.when(pl.program_id(0) == 0)
    def _():
        total = jnp.zeros((rows, 1), jnp.float32)
        square = jnp.zeros((rows, 1), jnp.float32)
        for t in range(shards):
            x = x_ref[t].astype(jnp.float32)
            total += jnp.sum(x, axis=1, keepdims=True)
            square += jnp.sum(x * x, axis=1, keepdims=True)
        mean = total / (shards * width)
        inverse = lax.rsqrt(square / (shards * width) - mean * mean + EPSILON)
        for t in range(shards):
            columns = slice(t * width, (t + 1) * width)
            x = x_ref[t].astype(jnp.float32)
            y = (x - mean) * inverse * (1.0 + scale_ref[:, columns]) + shift_ref[:, columns]
            normed_ref[:, columns] = y.astype(jnp.bfloat16)

    normed = normed_ref[...]

    def head_norm(shaped, gain):
        power = jnp.mean(shaped * shaped, axis=-1, keepdims=True)
        return (shaped * lax.rsqrt(power + EPSILON) * gain).astype(jnp.bfloat16)

    q = jnp.dot(normed, wq_ref[...], preferred_element_type=jnp.float32)
    k = jnp.dot(normed, wk_ref[...], preferred_element_type=jnp.float32)
    v = jnp.dot(normed, wv_ref[...], preferred_element_type=jnp.float32).astype(jnp.bfloat16)
    for h in range(heads):
        columns = slice(h * HEAD_DIM, (h + 1) * HEAD_DIM)
        q_ref[h] = head_norm(q[:, columns], qg_ref[h])
        kv_ref[0, h] = head_norm(k[:, columns], kg_ref[h])
        kv_ref[1, h] = v[:, columns]


def qkv(x, shift, scale, wq, wk, wv, qg, kg):
    shards, rows, width = x.shape
    model = shards * width
    heads = wq.shape[1] // HEAD_DIM
    step = 2 if heads % 2 == 0 else 1
    weight = pl.BlockSpec((model, step * HEAD_DIM), lambda h: (0, h))
    gain = pl.BlockSpec((step, 1, HEAD_DIM), lambda h: (h, 0, 0))
    row = pl.BlockSpec((1, model), lambda h: (0, 0))
    return pl.pallas_call(
        qkv_kernel,
        grid=(heads // step,),
        in_specs=[pl.BlockSpec((shards, rows, width), lambda h: (0, 0, 0)), row, row, weight, weight, weight, gain, gain],
        out_specs=[
            pl.BlockSpec((step, rows, HEAD_DIM), lambda h: (h, 0, 0)),
            pl.BlockSpec((2, step, rows, HEAD_DIM), lambda h: (0, h, 0, 0)),
        ],
        out_shape=[
            jax.ShapeDtypeStruct((heads, rows, HEAD_DIM), jnp.bfloat16),
            jax.ShapeDtypeStruct((2, heads, rows, HEAD_DIM), jnp.bfloat16),
        ],
        scratch_shapes=[pltpu.VMEM((rows, model), jnp.bfloat16)],
        compiler_params=pltpu.CompilerParams(vmem_limit_bytes=VMEM_BYTES),
        cost_estimate=pl.CostEstimate(
            flops=6 * rows * model * heads * HEAD_DIM, bytes_accessed=6 * model * heads * HEAD_DIM, transcendentals=0
        ),
    )(x, shift, scale, wq, wk, wv, qg[:, None, :], kg[:, None, :])


def attend_kernel(sources, parts, live_ref, *refs):
    q_refs = refs[: parts[0]]
    kv_refs = refs[parts[0] : parts[0] + sources * parts[1]]
    o_ref, max_ref, sum_ref, acc_ref = refs[parts[0] + sources * parts[1] :]
    q = jnp.concatenate([r[0] for r in q_refs], axis=0)
    part_rows = kv_refs[0].shape[2]
    block = part_rows * parts[1]

    def fold(s, first):
        mine = kv_refs[s * parts[1] : (s + 1) * parts[1]]
        live = live_ref[s]
        keys = jnp.concatenate([r[0, 0] for r in mine], axis=0)
        values = jnp.concatenate([r[1, 0] for r in mine], axis=0)
        scores = lax.dot_general(q, keys, (((1,), (1,)), ((), ())), preferred_element_type=jnp.float32)
        slot = lax.broadcasted_iota(jnp.int32, (1, block), 1)
        scores = jnp.where(slot < live, scores, NEG_FILL)
        top = jnp.max(scores, axis=1, keepdims=True)
        if not first:
            old = max_ref[:, :1]
            top = jnp.maximum(top, old)
            factor = jnp.exp2((old - top) * FACTOR)
        weights = jnp.exp2((scores - top) * FACTOR)
        total = weights[:, :HEAD_DIM]
        for i in range(1, block // HEAD_DIM):
            total += weights[:, i * HEAD_DIM : (i + 1) * HEAD_DIM]
        product = jnp.dot(weights.astype(jnp.bfloat16), values, preferred_element_type=jnp.float32)
        if first:
            sum_ref[...] = total
            acc_ref[...] = product
        else:
            sum_ref[...] = sum_ref[...] * factor + total
            acc_ref[...] = acc_ref[...] * factor + product
        max_ref[...] = jnp.broadcast_to(top, max_ref.shape)

    fold(0, True)
    for s in range(1, sources):
        pl.when(live_ref[s] > 0)(functools.partial(fold, s, False))
    o_ref[...] = (acc_ref[...] / jnp.sum(sum_ref[...], axis=1, keepdims=True)).astype(jnp.bfloat16)


def attend(live, queries, pieces):
    sources, key_parts = len(pieces), len(pieces[0])
    heads, part_rows, _ = queries[0].shape
    rows = part_rows * len(queries)
    q_spec = pl.BlockSpec((1, part_rows, HEAD_DIM), lambda h, live: (h, 0, 0))
    kv_spec = pl.BlockSpec((2, 1, pieces[0][0].shape[2], HEAD_DIM), lambda h, live: (0, h, 0, 0))
    flat = [p for piece in pieces for p in piece]
    keys = sources * key_parts * pieces[0][0].shape[2]
    return pl.pallas_call(
        functools.partial(attend_kernel, sources, (len(queries), key_parts)),
        grid_spec=pltpu.PrefetchScalarGridSpec(
            num_scalar_prefetch=1,
            grid=(heads,),
            in_specs=[q_spec] * len(queries) + [kv_spec] * len(flat),
            out_specs=pl.BlockSpec((rows, HEAD_DIM), lambda h, live: (0, h)),
            scratch_shapes=[pltpu.VMEM((rows, HEAD_DIM), jnp.float32)] * 3,
        ),
        out_shape=jax.ShapeDtypeStruct((rows, heads * HEAD_DIM), jnp.bfloat16),
        compiler_params=pltpu.CompilerParams(vmem_limit_bytes=VMEM_BYTES),
        cost_estimate=pl.CostEstimate(
            flops=4 * rows * keys * heads * HEAD_DIM,
            bytes_accessed=4 * keys * heads * HEAD_DIM,
            transcendentals=rows * keys * heads,
        ),
    )(live, *queries, *flat)


def on_device(
    latents,
    w_query,
    w_key,
    w_value,
    w_out,
    query_gain,
    key_gain,
    mod_table,
    levels,
    span_counts,
    block_mask,
    span_order,
):
    row_count, shard_width = latents.shape
    spans = lax.axis_size("frame")
    me = lax.axis_index("frame")
    column_start = lax.axis_index("tensor") * shard_width
    modulation = lax.dynamic_index_in_dim(mod_table, levels[0], 0, keepdims=False)
    shift_row, scale_row, gate_row = modulation[0:1], modulation[1:2], modulation[2]

    def from_ahead(block, distance):
        return lax.ppermute(block, "frame", [((i + distance) % spans, i) for i in range(spans)])

    part_rows = row_count // GATHER_PARTS
    queries, pieces = [], [[] for _ in range(spans)]
    for c in range(GATHER_PARTS):
        block = latents[c * part_rows : (c + 1) * part_rows]
        x = lax.all_gather(block, "tensor", axis=0)
        q, kv = qkv(x, shift_row, scale_row, w_query, w_key, w_value, query_gain, key_gain)
        queries.append(q)
        for s in range(spans):
            pieces[s].append(kv if s == 0 else None)
        for s in range(2, spans, 2):
            pieces[s][c] = from_ahead(kv, s)
        swapped = []
        for s in range(0, spans, 2):
            swapped.append(
                lax.ppermute(pieces[s][c], "frame", [(i ^ 1, i) for i in range(spans)])
            )
        for s in range(0, spans, 2):
            pieces[s + 1][c] = swapped[s // 2]

    offsets = jnp.arange(spans, dtype=jnp.int32)
    span_of = lax.rem(jnp.where(offsets % 2 == 0, me, me ^ 1) + offsets // 2 * 2, spans)
    own = offsets == 0
    allowed = (span_order[span_of] <= span_order[me]) & ((block_mask[0][span_of] == 1) | own)
    live = jnp.where(allowed, span_counts[span_of], 0).astype(jnp.int32)

    gate_part = lax.dynamic_slice_in_dim(gate_row, column_start, shard_width)
    per = GATHER_PARTS // QUERY_PARTS
    results = []
    for c in range(QUERY_PARTS):
        attended = attend(live, queries[c * per : (c + 1) * per], pieces)
        partial_out = jnp.dot(attended, w_out, preferred_element_type=jnp.float32).astype(jnp.bfloat16)
        projected = lax.psum_scatter(partial_out, "tensor", scatter_dimension=1, tiled=True).astype(jnp.float32)
        rows = latents[c * per * part_rows : (c + 1) * per * part_rows].astype(jnp.float32)
        results.append((rows + gate_part * projected).astype(jnp.bfloat16))
    return jnp.concatenate(results, axis=0)


def solution(mesh):
    return jax.shard_map(
        on_device,
        mesh=mesh,
        in_specs=(
            P("frame", "tensor"),
            P(None, "tensor"),
            P(None, "tensor"),
            P(None, "tensor"),
            P("tensor", None),
            P("tensor", None),
            P("tensor", None),
            P(),
            P("frame"),
            P(),
            P("frame", None),
            P(),
        ),
        out_specs=P("frame", "tensor"),
        check_vma=False,
    )
```

time: 479 us -> 355 us (0.74)
  waiting for transfers between devices: 307 us -> 204 us
  Pallas kernels: 0 us -> 85.6 us
  matrix products: 66.1 us -> 14.1 us
  other arithmetic: 47.1 us -> 3.56 us
  starting transfers between devices: 0.11 us -> 18.7 us
  local copies, waits for them, and re-layouts: 27.2 us -> 11.7 us
  loops' own time: 13.6 us -> 0 us
    ppermute x7 -> x28, waiting for transfers between devices: 120 us -> 30.5 us  [the longest x12 29.4 us: from_ahead(): lax.ppermute(block, 'frame', [((i + distance) % spans, i) for i in range(...]
    pallas_call x0 -> x6, Pallas kernels: none -> 85.6 us  [the longest x4 49.2 us: qkv(): pl.pallas_call(qkv_kernel, grid=(heads // step,), in_specs=[pl.BlockSpec(...]
    dot_general x20 -> x2, matrix products: 66.1 us -> 14.1 us  [on_device(): jnp.dot(attended, w_out, preferred_element_type=jnp.float32)]
    reduce_sum x28 -> x0, other arithmetic: 31 us -> none  [the longest x8 13.4 us: fold_block(): new_sum = running_sum * factor + jnp.sum(weights, axis=-1)]
    ppermute x7 -> x28, starting transfers between devices: 0.07 us -> 18.3 us  [the longest x12 15.4 us: from_ahead(): lax.ppermute(block, 'frame', [((i + distance) % spans, i) for i in range(...]
    while x43 -> x0, local copies, waits for them, and re-layouts: 13.7 us -> none
    another operation x1 -> x0, loops' own time: 13.6 us -> none  [on_device(): lax.fori_loop(1, span_total, hand_over, (carried, kv_pair))]
    all_gather x1 -> x4, waiting for transfers between devices: 95 us -> 83.7 us  [on_device(): x = lax.all_gather(block, 'tensor', axis=0)]
  transfers between devices with their start and end apart: 9 -> 34, of which waited for: 9 -> 12; matrix products, arithmetic and copies ran while one was open for 4% -> 5% of each run, Pallas kernels for 0% -> 19%
where the time goes in v1:
time: 355 us; the launch traced here: 352 us
  waiting for transfers between devices  204 us (57%)
  Pallas kernels  85.6 us (24%)
  starting transfers between devices  18.7 us (5%)
  between operations  14.4 us (4%)
  matrix products  14.1 us (4%)
  local copies, waits for them, and re-layouts  11.7 us (3%)
  other arithmetic  3.56 us (1%)
    reduce_scatter x2, waiting for transfers between devices, on_device(): lax.psum_scatter(partial_out, 'tensor', scatter_dimension=1, tiled=True)  87.9 us
    all_gather x4, waiting for transfers between devices, on_device(): x = lax.all_gather(block, 'tensor', axis=0)  83.7 us
    pallas_call x4, Pallas kernels, qkv(): pl.pallas_call(qkv_kernel, grid=(heads // step,), in_specs=[pl.BlockSpec(...  49.2 us
    pallas_call x2, Pallas kernels, attend(): pl.pallas_call(functools.partial(attend_kernel, sources, (len(queries), k...  36.3 us
    ppermute x12, waiting for transfers between devices, from_ahead(): lax.ppermute(block, 'frame', [((i + distance) % spans, i) for i in range(...  29.4 us
    ppermute x12, starting transfers between devices, from_ahead(): lax.ppermute(block, 'frame', [((i + distance) % spans, i) for i in range(...  15.4 us
    dot_general x2, matrix products, on_device(): jnp.dot(attended, w_out, preferred_element_type=jnp.float32)  14.1 us
  transfers between devices with their start and end apart: 34, of which 12 were waited for; matrix products, arithmetic and copies ran while one was open for 5% of the time, Pallas kernels for 19%

profile of v1, /device:TPU:0, one launch (start us, length us, event | category | flops | bytes accessed | tf_op | source)
XLA Modules:
  0.0 352.2 jit_solution(13673634377358259651)
XLA Ops:
  6.5 2.3 fusion.4
  9.0 0.7 all-gather.9.cloned.1.call-update
  9.7 0.7 all-gather.11.cloned.1.call-update
  10.4 0.5 all-gather.13.cloned.1.call-update
  11.7 0.6 broadcast_in_dim.15.qg_ref
  12.3 0.6 broadcast_in_dim.17.kg_ref
  12.9 1.6 dynamic-slice_bitcast_fusion
  14.5 29.9 %all-gather.15.cloned.1.call-done = bf16[512,1280]{1,0:T(8,128)(2,1)} async-done(((bf16[128,1280]{1,0:T(8,128)(2,1)}), bf16[512,1280]{1,0:T(8,128)(2,1)}) %all-gather.15.cloned.1.call-update) | async-done | bytes 1310736 | tf_op jit(solution)/shard_map/all_gather | solution.py:179
  44.5 12.4 %shard_map.121 = (bf16[6,128,128]{2,1,0:T(8,128)(2,1)}, bf16[2,6,128,128]{3,2,1,0:T(8,128)(2,1)}) custom-call(bf16[4,128,1280]{2,1,0:T(8,128)(2,1)} %bitcast.24, f32[1,5120]{1,0:T(1,128)} %get-tuple-element.28.shift_ref, f32[1,5120]{1,0:T(1,128)} %get-tuple-element.27.scale_ref, bf16[5120,768]{1,0:T(8,128)(2,1)} %wq_ref.7, bf16[5120,768]{1,0:T(8,128)(2,1)} %wk_ref.7, ...), custom_call_target="tpu_custom_call" | custom-call | flops 3019898880 | bytes 23592960 | tf_op jit(solution)/shard_map/pallas_call | solution.py:64
  56.8 1.5 collective-permute-start.23
  58.3 1.5 collective-permute-start.15
  59.8 1.5 collective-permute-start.7
  61.3 16.5 %all-gather.9.cloned.1.call-done = bf16[512,1280]{1,0:T(8,128)(2,1)} async-done(((bf16[128,1280]{1,0:T(8,128)(2,1)}), bf16[512,1280]{1,0:T(8,128)(2,1)}) %all-gather.9.cloned.1.call-update) | async-done | bytes 1310736 | tf_op jit(solution)/shard_map/all_gather | solution.py:179
  77.7 12.4 %shard_map.118 = (bf16[6,128,128]{2,1,0:T(8,128)(2,1)}, bf16[2,6,128,128]{3,2,1,0:T(8,128)(2,1)}) custom-call(bf16[4,128,1280]{2,1,0:T(8,128)(2,1)} %bitcast.23, f32[1,5120]{1,0:T(1,128)} %get-tuple-element.28.shift_ref, f32[1,5120]{1,0:T(1,128)} %get-tuple-element.27.scale_ref, bf16[5120,768]{1,0:T(8,128)(2,1)} %wq_ref.7, bf16[5120,768]{1,0:T(8,128)(2,1)} %wk_ref.7, ...), custom_call_target="tpu_custom_call" | custom-call | flops 3019898880 | bytes 23592960 | tf_op jit(solution)/shard_map/pallas_call | solution.py:64
  90.1 1.5 collective-permute-start.20
  91.6 1.5 collective-permute-start.12
  93.1 1.5 collective-permute-start.4
  94.6 16.5 %all-gather.11.cloned.1.call-done = bf16[512,1280]{1,0:T(8,128)(2,1)} async-done(((bf16[128,1280]{1,0:T(8,128)(2,1)}), bf16[512,1280]{1,0:T(8,128)(2,1)}) %all-gather.11.cloned.1.call-update) | async-done | bytes 1310736 | tf_op jit(solution)/shard_map/all_gather | solution.py:179
  111.0 12.3 %shard_map.119 = (bf16[6,128,128]{2,1,0:T(8,128)(2,1)}, bf16[2,6,128,128]{3,2,1,0:T(8,128)(2,1)}) custom-call(bf16[4,128,1280]{2,1,0:T(8,128)(2,1)} %bitcast.21, f32[1,5120]{1,0:T(1,128)} %get-tuple-element.28.shift_ref, f32[1,5120]{1,0:T(1,128)} %get-tuple-element.27.scale_ref, bf16[5120,768]{1,0:T(8,128)(2,1)} %wq_ref.7, bf16[5120,768]{1,0:T(8,128)(2,1)} %wk_ref.7, ...), custom_call_target="tpu_custom_call" | custom-call | flops 3019898880 | bytes 23592960 | tf_op jit(solution)/shard_map/pallas_call | solution.py:64
  123.4 20.8 %all-gather.13.cloned.1.call-done = bf16[512,1280]{1,0:T(8,128)(2,1)} async-done(((bf16[128,1280]{1,0:T(8,128)(2,1)}), bf16[512,1280]{1,0:T(8,128)(2,1)}) %all-gather.13.cloned.1.call-update) | async-done | bytes 1310736 | tf_op jit(solution)/shard_map/all_gather | solution.py:179
  144.2 12.2 %shard_map.120 = (bf16[6,128,128]{2,1,0:T(8,128)(2,1)}, bf16[2,6,128,128]{3,2,1,0:T(8,128)(2,1)}) custom-call(bf16[4,128,1280]{2,1,0:T(8,128)(2,1)} %bitcast.22, f32[1,5120]{1,0:T(1,128)} %get-tuple-element.28.shift_ref, f32[1,5120]{1,0:T(1,128)} %get-tuple-element.27.scale_ref, bf16[5120,768]{1,0:T(8,128)(2,1)} %wq_ref.7, bf16[5120,768]{1,0:T(8,128)(2,1)} %wk_ref.7, ...), custom_call_target="tpu_custom_call" | custom-call | flops 3019898880 | bytes 23592960 | tf_op jit(solution)/shard_map/pallas_call | solution.py:64
  156.4 1.5 collective-permute-start.22
  157.9 1.5 collective-permute-start.14
  159.4 1.5 collective-permute-start.6
  160.9 0.6 collective-permute-start.21
  161.5 8.2 %collective-permute-done.22.refs_28_ = bf16[2,6,128,128]{3,2,1,0:T(8,128)(2,1)} collective-permute-done((bf16[2,6,128,128]{3,2,1,0:T(8,128)(2,1)}, bf16[2,6,128,128]{3,2,1,0:T(8,128)(2,1)}, u32[]{:S(2)}, u32[]{:S(2)}) %collective-permute-start.22) | collective-permute-done | bytes 393248 | tf_op jit(solution)/shard_map/ppermute | solution.py:173
  169.7 1.5 collective-permute-start.13
  171.2 6.9 %collective-permute-done.14.refs_20_ = bf16[2,6,128,128]{3,2,1,0:T(8,128)(2,1)S(1)} collective-permute-done((bf16[2,6,128,128]{3,2,1,0:T(8,128)(2,1)}, bf16[2,6,128,128]{3,2,1,0:T(8,128)(2,1)S(1)}, u32[]{:S(2)}, u32[]{:S(2)}) %collective-permute-start.14) | collective-permute-done | bytes 393248 | tf_op jit(solution)/shard_map/ppermute | solution.py:173
  178.2 0.5 collective-permute-start.27
  178.8 7.7 %collective-permute-done.21.refs_27_ = bf16[2,6,128,128]{3,2,1,0:T(8,128)(2,1)S(1)} collective-permute-done((bf16[2,6,128,128]{3,2,1,0:T(8,128)(2,1)S(1)}, bf16[2,6,128,128]{3,2,1,0:T(8,128)(2,1)S(1)}, u32[]{:S(2)}, u32[]{:S(2)}) %collective-permute-start.21) | collective-permute-done | bytes 393248 | tf_op jit(solution)/shard_map/ppermute | solution.py:173
  186.5 6.5 %collective-permute-done.13.refs_19_ = bf16[2,6,128,128]{3,2,1,0:T(8,128)(2,1)S(1)} collective-permute-done((bf16[2,6,128,128]{3,2,1,0:T(8,128)(2,1)S(1)}, bf16[2,6,128,128]{3,2,1,0:T(8,128)(2,1)S(1)}, u32[]{:S(2)}, u32[]{:S(2)}) %collective-permute-start.13) | collective-permute-done | bytes 393248 | tf_op jit(solution)/shard_map/ppermute | solution.py:173
  194.4 0.4 copy-done.21
  194.9 0.7 dynamic_slice.12
  196.1 1.1 collective-permute-done.16.refs_22_
  197.8 1.2 gather_fusion
  199.0 0.6 gather_fusion.2
  199.6 0.6 gather_fusion.1
  200.3 1.9 and_select_fusion.live_ref
  202.3 0.6 copy-done.24
  202.9 18.1 %shard_map.122 = bf16[256,768]{1,0:T(8,128)(2,1)} custom-call(s32[8]{0:T(128)} %and_select_fusion.live_ref, bf16[6,128,128]{2,1,0:T(8,128)(2,1)} %get-tuple-element.13.refs_0_, bf16[6,128,128]{2,1,0:T(8,128)(2,1)} %get-tuple-element.14.refs_1_, bf16[2,6,128,128]{3,2,1,0:T(8,128)(2,1)} %get-tuple-element.15.refs_2_, ...), custom_call_target="tpu_custom_call" | custom-call | flops 3221225472 | bytes 12582912 | tf_op jit(solution)/shard_map/pallas_call | solution.py:132
  221.0 7.1 %convolution_convert_fusion.1 = bf16[256,5120]{1,0:T(8,128)(2,1)} fusion(bf16[256,768]{1,0:T(8,128)(2,1)} %shard_map.122, bf16[768,5120]{1,0:T(8,128)(2,1)} %param.16), kind=kOutput, calls=%fused_computation.4 | convolution fusion | flops 2014576640 | bytes 10878976 | tf_op jit(solution)/shard_map/dot_general | solution.py:205
  228.4 18.2 %shard_map.123 = bf16[256,768]{1,0:T(8,128)(2,1)} custom-call(s32[8]{0:T(128)} %and_select_fusion.live_ref, bf16[6,128,128]{2,1,0:T(8,128)(2,1)} %get-tuple-element.19.refs_0_, bf16[6,128,128]{2,1,0:T(8,128)(2,1)} %get-tuple-element.20.refs_1_, bf16[2,6,128,128]{3,2,1,0:T(8,128)(2,1)} %get-tuple-element.15.refs_2_, ...), custom_call_target="tpu_custom_call" | custom-call | flops 3221225472 | bytes 12582912 | tf_op jit(solution)/shard_map/pallas_call | solution.py:132
  246.6 7.1 %convolution_convert_fusion = bf16[256,5120]{1,0:T(8,128)(2,1)} fusion(bf16[256,768]{1,0:T(8,128)(2,1)} %shard_map.123, bf16[768,5120]{1,0:T(8,128)(2,1)} %param.16), kind=kOutput, calls=%fused_computation.3 | convolution fusion | flops 2014576640 | bytes 10878976 | tf_op jit(solution)/shard_map/dot_general | solution.py:205
  253.7 1.0 dynamic-slice_reduce_fusion
  254.7 33.9 %reduce-scatter.3.cloned.1.call-done = bf16[256,1280]{1,0:T(8,128)(2,1)} async-done(((bf16[256,5120]{1,0:T(8,128)(2,1)}), bf16[256,1280]{1,0:T(8,128)(2,1)}) %reduce-scatter.3.cloned.1.call-update) | async-done | bytes 655376 | tf_op jit(solution)/shard_map/reduce_scatter | solution.py:206
  288.6 54.0 %reduce-scatter.5.cloned.1.call-done = bf16[256,1280]{1,0:T(8,128)(2,1)} async-done(((bf16[256,5120]{1,0:T(8,128)(2,1)}), bf16[256,1280]{1,0:T(8,128)(2,1)}) %reduce-scatter.5.cloned.1.call-update) | async-done | bytes 655376 | tf_op jit(solution)/shard_map/reduce_scatter | solution.py:206
  342.6 1.7 add_convert_fusion.1
  344.3 1.0 copy-done.27
  (104 shorter events, 3.3 us)
Async XLA Ops:
  6.5 193.1 %copy-start = (s32[1,8]{1,0:T(1,128)S(1)}, s32[1,8]{1,0:T(1,128)}, u32[]{:S(2)}) copy-start(s32[1,8]{1,0:T(1,128)} %param.22) | copy-start | bytes 100
  6.5 37.9 %all-gather.15.cloned.1.call-start = ((), (), s32[]{:S(2)}) async-start(), calls=%async_computation.7 | async-start | bytes 1638400 | tf_op jit(solution)/shard_map/all_gather | solution.py:179
  8.9 68.8 %all-gather.9.cloned.1.call-start = ((), (), s32[]{:S(2)}) async-start(), calls=%async_computation.4 | async-start | bytes 1638400 | tf_op jit(solution)/shard_map/all_gather | solution.py:179
  9.7 101.4 %all-gather.11.cloned.1.call-start = ((), (), s32[]{:S(2)}) async-start(), calls=%async_computation.5 | async-start | bytes 1638400 | tf_op jit(solution)/shard_map/all_gather | solution.py:179
  10.4 133.8 %all-gather.13.cloned.1.call-start = ((), (), s32[]{:S(2)}) async-start(), calls=%async_computation.6 | async-start | bytes 1638400 | tf_op jit(solution)/shard_map/all_gather | solution.py:179
  11.0 277.6 %reduce-scatter.3.cloned.1.call-start = ((), (), s32[]{:S(2)}) async-start(), calls=%async_computation.2 | async-start | bytes 3276800 | tf_op jit(solution)/shard_map/reduce_scatter | solution.py:206
  56.8 34.8 %collective-permute-start.23 = (bf16[2,6,128,128]{3,2,1,0:T(8,128)(2,1)}, bf16[2,6,128,128]{3,2,1,0:T(8,128)(2,1)S(1)}, u32[]{:S(2)}, u32[]{:S(2)}) collective-permute-start(bf16[2,6,128,128]{3,2,1,0:T(8,128)(2,1)} %get-tuple-element.18.refs_5_), channel_id=1, source_target_pairs={{24,0},{28,4},{0,8},{4,12},{8,16},{12,20},{16,24},{20,28},{25,1},{... | collective-permute-start | bytes 1179656 | tf_op jit(solution)/shard_map/ppermute | solution.py:173
  58.3 34.8 %collective-permute-start.15 = (bf16[2,6,128,128]{3,2,1,0:T(8,128)(2,1)}, bf16[2,6,128,128]{3,2,1,0:T(8,128)(2,1)S(1)}, u32[]{:S(2)}, u32[]{:S(2)}) collective-permute-start(bf16[2,6,128,128]{3,2,1,0:T(8,128)(2,1)} %get-tuple-element.18.refs_5_), channel_id=1, source_target_pairs={{16,0},{20,4},{24,8},{28,12},{0,16},{4,20},{8,24},{12,28},{17,1},{... | collective-permute-start | bytes 1179656 | tf_op jit(solution)/shard_map/ppermute | solution.py:173
  59.8 34.8 %collective-permute-start.7 = (bf16[2,6,128,128]{3,2,1,0:T(8,128)(2,1)}, bf16[2,6,128,128]{3,2,1,0:T(8,128)(2,1)S(1)}, u32[]{:S(2)}, u32[]{:S(2)}) collective-permute-start(bf16[2,6,128,128]{3,2,1,0:T(8,128)(2,1)} %get-tuple-element.18.refs_5_), channel_id=1, source_target_pairs={{8,0},{12,4},{16,8},{20,12},{24,16},{28,20},{0,24},{4,28},{9,1},{1... | collective-permute-start | bytes 1179656 | tf_op jit(solution)/shard_map/ppermute | solution.py:173
  61.3 95.1 %collective-permute-start.3 = (bf16[2,6,128,128]{3,2,1,0:T(8,128)(2,1)}, bf16[2,6,128,128]{3,2,1,0:T(8,128)(2,1)S(1)}, u32[]{:S(2)}, u32[]{:S(2)}) collective-permute-start(bf16[2,6,128,128]{3,2,1,0:T(8,128)(2,1)} %get-tuple-element.18.refs_5_), channel_id=1, source_target_pairs={{4,0},{0,4},{12,8},{8,12},{20,16},{16,20},{28,24},{24,28},{5,1},{1... | collective-permute-start | bytes 1179656 | tf_op jit(solution)/shard_map/ppermute | solution.py:189
  90.1 67.8 %collective-permute-start.20 = (bf16[2,6,128,128]{3,2,1,0:T(8,128)(2,1)}, bf16[2,6,128,128]{3,2,1,0:T(8,128)(2,1)S(1)}, u32[]{:S(2)}, u32[]{:S(2)}) collective-permute-start(bf16[2,6,128,128]{3,2,1,0:T(8,128)(2,1)} %get-tuple-element.15.refs_2_), channel_id=1, source_target_pairs={{24,0},{28,4},{0,8},{4,12},{8,16},{12,20},{16,24},{20,28},{25,1},{... | collective-permute-start | bytes 1179656 | tf_op jit(solution)/shard_map/ppermute | solution.py:173
  91.6 86.6 %copy-start.4 = (bf16[2,6,128,128]{3,2,1,0:T(8,128)(2,1)}, bf16[2,6,128,128]{3,2,1,0:T(8,128)(2,1)S(1)}, u32[]{:S(2)}) copy-start(bf16[2,6,128,128]{3,2,1,0:T(8,128)(2,1)S(1)} %collective-permute-done.23.refs_29_) | copy-start | bytes 1179652
  91.6 67.8 %collective-permute-start.12 = (bf16[2,6,128,128]{3,2,1,0:T(8,128)(2,1)}, bf16[2,6,128,128]{3,2,1,0:T(8,128)(2,1)S(1)}, u32[]{:S(2)}, u32[]{:S(2)}) collective-permute-start(bf16[2,6,128,128]{3,2,1,0:T(8,128)(2,1)} %get-tuple-element.15.refs_2_), channel_id=1, source_target_pairs={{16,0},{20,4},{24,8},{28,12},{0,16},{4,20},{8,24},{12,28},{17,1},{... | collective-permute-start | bytes 1179656 | tf_op jit(solution)/shard_map/ppermute | solution.py:173
  93.1 93.4 %copy-start.5 = (bf16[2,6,128,128]{3,2,1,0:T(8,128)(2,1)}, bf16[2,6,128,128]{3,2,1,0:T(8,128)(2,1)S(1)}, u32[]{:S(2)}) copy-start(bf16[2,6,128,128]{3,2,1,0:T(8,128)(2,1)S(1)} %collective-permute-done.15.refs_21_) | copy-start | bytes 1179652
  93.1 67.7 %collective-permute-start.4 = (bf16[2,6,128,128]{3,2,1,0:T(8,128)(2,1)}, bf16[2,6,128,128]{3,2,1,0:T(8,128)(2,1)S(1)}, u32[]{:S(2)}, u32[]{:S(2)}) collective-permute-start(bf16[2,6,128,128]{3,2,1,0:T(8,128)(2,1)} %get-tuple-element.15.refs_2_), channel_id=1, source_target_pairs={{8,0},{12,4},{16,8},{20,12},{24,16},{28,20},{0,24},{4,28},{9,1},{1... | collective-permute-start | bytes 1179656 | tf_op jit(solution)/shard_map/ppermute | solution.py:173
  94.6 98.5 %copy-start.6 = (bf16[2,6,128,128]{3,2,1,0:T(8,128)(2,1)}, bf16[2,6,128,128]{3,2,1,0:T(8,128)(2,1)S(1)}, u32[]{:S(2)}) copy-start(bf16[2,6,128,128]{3,2,1,0:T(8,128)(2,1)S(1)} %collective-permute-done.7.refs_13_) | copy-start | bytes 1179652
  94.6 66.3 %collective-permute-start = (bf16[2,6,128,128]{3,2,1,0:T(8,128)(2,1)}, bf16[2,6,128,128]{3,2,1,0:T(8,128)(2,1)S(1)}, u32[]{:S(2)}, u32[]{:S(2)}) collective-permute-start(bf16[2,6,128,128]{3,2,1,0:T(8,128)(2,1)} %get-tuple-element.15.refs_2_), channel_id=1, source_target_pairs={{4,0},{0,4},{12,8},{8,12},{20,16},{16,20},{28,24},{24,28},{5,1},{1... | collective-permute-start | bytes 1179656 | tf_op jit(solution)/shard_map/ppermute | solution.py:189
  144.2 16.7 %copy-start.12 = (bf16[2,6,128,128]{3,2,1,0:T(8,128)(2,1)S(1)}, bf16[2,6,128,128]{3,2,1,0:T(8,128)(2,1)}, u32[]{:S(2)}) copy-start(bf16[2,6,128,128]{3,2,1,0:T(8,128)(2,1)} %get-tuple-element.16.refs_3_) | copy-start | bytes 1179652
  144.2 50.7 %copy-start.1 = (s32[8]{0:T(128)S(1)}, s32[8]{0:T(128)}, u32[]{:S(2)}) copy-start(s32[8]{0:T(128)} %param.23) | copy-start | bytes 100
  144.2 54.8 %copy-start.2 = (s32[8]{0:T(128)S(1)}, s32[8]{0:T(128)}, u32[]{:S(2)}) copy-start(s32[8]{0:T(128)} %param.21) | copy-start | bytes 100
  156.4 45.8 %copy-start.7 = (bf16[2,6,128,128]{3,2,1,0:T(8,128)(2,1)}, bf16[2,6,128,128]{3,2,1,0:T(8,128)(2,1)S(1)}, u32[]{:S(2)}) copy-start(bf16[2,6,128,128]{3,2,1,0:T(8,128)(2,1)S(1)} %collective-permute-done.3.refs_9_) | copy-start | bytes 1179652
  156.4 13.4 %collective-permute-start.22 = (bf16[2,6,128,128]{3,2,1,0:T(8,128)(2,1)}, bf16[2,6,128,128]{3,2,1,0:T(8,128)(2,1)}, u32[]{:S(2)}, u32[]{:S(2)}) collective-permute-start(bf16[2,6,128,128]{3,2,1,0:T(8,128)(2,1)} %get-tuple-element.17.refs_4_), channel_id=1, source_target_pairs={{24,0},{28,4},{0,8},{4,12},{8,16},{12,20},{16,24},{20,28},{25,1},{... | collective-permute-start | bytes 1179656 | tf_op jit(solution)/shard_map/ppermute | solution.py:173
  157.9 44.3 %copy-start.8 = (bf16[2,6,128,128]{3,2,1,0:T(8,128)(2,1)}, bf16[2,6,128,128]{3,2,1,0:T(8,128)(2,1)S(1)}, u32[]{:S(2)}) copy-start(bf16[2,6,128,128]{3,2,1,0:T(8,128)(2,1)S(1)} %collective-permute-done.20.refs_26_) | copy-start | bytes 1179652
  157.9 20.2 %collective-permute-start.14 = (bf16[2,6,128,128]{3,2,1,0:T(8,128)(2,1)}, bf16[2,6,128,128]{3,2,1,0:T(8,128)(2,1)S(1)}, u32[]{:S(2)}, u32[]{:S(2)}) collective-permute-start(bf16[2,6,128,128]{3,2,1,0:T(8,128)(2,1)} %get-tuple-element.17.refs_4_), channel_id=1, source_target_pairs={{16,0},{20,4},{24,8},{28,12},{0,16},{4,20},{8,24},{12,28},{17,1},{... | collective-permute-start | bytes 1179656 | tf_op jit(solution)/shard_map/ppermute | solution.py:173
  159.4 42.8 %copy-start.9 = (bf16[2,6,128,128]{3,2,1,0:T(8,128)(2,1)}, bf16[2,6,128,128]{3,2,1,0:T(8,128)(2,1)S(1)}, u32[]{:S(2)}) copy-start(bf16[2,6,128,128]{3,2,1,0:T(8,128)(2,1)S(1)} %collective-permute-done.12.refs_18_) | copy-start | bytes 1179652
  159.4 18.7 %collective-permute-start.6 = (bf16[2,6,128,128]{3,2,1,0:T(8,128)(2,1)}, bf16[2,6,128,128]{3,2,1,0:T(8,128)(2,1)S(1)}, u32[]{:S(2)}, u32[]{:S(2)}) collective-permute-start(bf16[2,6,128,128]{3,2,1,0:T(8,128)(2,1)} %get-tuple-element.17.refs_4_), channel_id=1, source_target_pairs={{8,0},{12,4},{16,8},{20,12},{24,16},{28,20},{0,24},{4,28},{9,1},{1... | collective-permute-start | bytes 1179656 | tf_op jit(solution)/shard_map/ppermute | solution.py:173
  160.8 41.4 %copy-start.10 = (bf16[2,6,128,128]{3,2,1,0:T(8,128)(2,1)}, bf16[2,6,128,128]{3,2,1,0:T(8,128)(2,1)S(1)}, u32[]{:S(2)}) copy-start(bf16[2,6,128,128]{3,2,1,0:T(8,128)(2,1)S(1)} %collective-permute-done.4.refs_10_) | copy-start | bytes 1179652
  160.8 17.4 %collective-permute-start.2 = (bf16[2,6,128,128]{3,2,1,0:T(8,128)(2,1)}, bf16[2,6,128,128]{3,2,1,0:T(8,128)(2,1)S(1)}, u32[]{:S(2)}, u32[]{:S(2)}) collective-permute-start(bf16[2,6,128,128]{3,2,1,0:T(8,128)(2,1)} %get-tuple-element.17.refs_4_), channel_id=1, source_target_pairs={{4,0},{0,4},{12,8},{8,12},{20,16},{16,20},{28,24},{24,28},{5,1},{1... | collective-permute-start | bytes 1179656 | tf_op jit(solution)/shard_map/ppermute | solution.py:189
  160.9 41.4 %copy-start.11 = (bf16[2,6,128,128]{3,2,1,0:T(8,128)(2,1)}, bf16[2,6,128,128]{3,2,1,0:T(8,128)(2,1)S(1)}, u32[]{:S(2)}) copy-start(bf16[2,6,128,128]{3,2,1,0:T(8,128)(2,1)S(1)} %collective-permute-done.refs_6_) | copy-start | bytes 1179652
  160.9 25.6 %collective-permute-start.21 = (bf16[2,6,128,128]{3,2,1,0:T(8,128)(2,1)S(1)}, bf16[2,6,128,128]{3,2,1,0:T(8,128)(2,1)S(1)}, u32[]{:S(2)}, u32[]{:S(2)}) collective-permute-start(bf16[2,6,128,128]{3,2,1,0:T(8,128)(2,1)S(1)} %copy-done.12), channel_id=1, source_target_pairs={{24,0},{28,4},{0,8},{4,12},{8,16},{12,20},{16,24},{20,28},{25,1},{... | collective-permute-start | bytes 1179656 | tf_op jit(solution)/shard_map/ppermute | solution.py:173
  169.7 23.3 %collective-permute-start.13 = (bf16[2,6,128,128]{3,2,1,0:T(8,128)(2,1)S(1)}, bf16[2,6,128,128]{3,2,1,0:T(8,128)(2,1)S(1)}, u32[]{:S(2)}, u32[]{:S(2)}) collective-permute-start(bf16[2,6,128,128]{3,2,1,0:T(8,128)(2,1)S(1)} %copy-done.12), channel_id=1, source_target_pairs={{16,0},{20,4},{24,8},{28,12},{0,16},{4,20},{8,24},{12,28},{17,1},{... | collective-permute-start | bytes 1179656 | tf_op jit(solution)/shard_map/ppermute | solution.py:173
  178.1 24.1 %copy-start.13 = (bf16[2,6,128,128]{3,2,1,0:T(8,128)(2,1)}, bf16[2,6,128,128]{3,2,1,0:T(8,128)(2,1)S(1)}, u32[]{:S(2)}) copy-start(bf16[2,6,128,128]{3,2,1,0:T(8,128)(2,1)S(1)} %collective-permute-done.14.refs_20_) | copy-start | bytes 1179652
  178.1 15.0 %collective-permute-start.5 = (bf16[2,6,128,128]{3,2,1,0:T(8,128)(2,1)S(1)}, bf16[2,6,128,128]{3,2,1,0:T(8,128)(2,1)S(1)}, u32[]{:S(2)}, u32[]{:S(2)}) collective-permute-start(bf16[2,6,128,128]{3,2,1,0:T(8,128)(2,1)S(1)} %copy-done.12), channel_id=1, source_target_pairs={{8,0},{12,4},{16,8},{20,12},{24,16},{28,20},{0,24},{4,28},{9,1},{1... | collective-permute-start | bytes 1179656 | tf_op jit(solution)/shard_map/ppermute | solution.py:173
  178.1 15.4 %collective-permute-start.1 = (bf16[2,6,128,128]{3,2,1,0:T(8,128)(2,1)S(1)}, bf16[2,6,128,128]{3,2,1,0:T(8,128)(2,1)S(1)}, u32[]{:S(2)}, u32[]{:S(2)}) collective-permute-start(bf16[2,6,128,128]{3,2,1,0:T(8,128)(2,1)S(1)} %copy-done.12), channel_id=1, source_target_pairs={{4,0},{0,4},{12,8},{8,12},{20,16},{16,20},{28,24},{24,28},{5,1},{1... | collective-permute-start | bytes 1179656 | tf_op jit(solution)/shard_map/ppermute | solution.py:189
  178.2 15.4 %collective-permute-start.27 = (bf16[2,6,128,128]{3,2,1,0:T(8,128)(2,1)S(1)}, bf16[2,6,128,128]{3,2,1,0:T(8,128)(2,1)S(1)}, u32[]{:S(2)}, u32[]{:S(2)}) collective-permute-start(bf16[2,6,128,128]{3,2,1,0:T(8,128)(2,1)S(1)} %collective-permute-done.23.refs_29_), channel_id=1, source_target_pairs={{4,0},{0,4},{12,8},{8,12},{20,16},{16,20},{28,24},{24,28},{5,1},{1... | collective-permute-start | bytes 1179656 | tf_op jit(solution)/shard_map/ppermute | solution.py:189
  186.5 7.5 %collective-permute-start.19 = (bf16[2,6,128,128]{3,2,1,0:T(8,128)(2,1)S(1)}, bf16[2,6,128,128]{3,2,1,0:T(8,128)(2,1)S(1)}, u32[]{:S(2)}, u32[]{:S(2)}) collective-permute-start(bf16[2,6,128,128]{3,2,1,0:T(8,128)(2,1)S(1)} %collective-permute-done.15.refs_21_), channel_id=1, source_target_pairs={{4,0},{0,4},{12,8},{8,12},{20,16},{16,20},{28,24},{24,28},{5,1},{1... | collective-permute-start | bytes 1179656 | tf_op jit(solution)/shard_map/ppermute | solution.py:189
  193.0 2.5 collective-permute-start.11
  193.1 2.6 collective-permute-start.24
  193.5 3.6 %collective-permute-start.16 = (bf16[2,6,128,128]{3,2,1,0:T(8,128)(2,1)S(1)}, bf16[2,6,128,128]{3,2,1,0:T(8,128)(2,1)}, u32[]{:S(2)}, u32[]{:S(2)}) collective-permute-start(bf16[2,6,128,128]{3,2,1,0:T(8,128)(2,1)S(1)} %collective-permute-done.12.refs_18_), channel_id=1, source_target_pairs={{4,0},{0,4},{12,8},{8,12},{20,16},{16,20},{28,24},{24,28},{5,1},{1... | collective-permute-start | bytes 1179656 | tf_op jit(solution)/shard_map/ppermute | solution.py:189
  193.6 3.6 %collective-permute-start.8 = (bf16[2,6,128,128]{3,2,1,0:T(8,128)(2,1)S(1)}, bf16[2,6,128,128]{3,2,1,0:T(8,128)(2,1)S(1)}, u32[]{:S(2)}, u32[]{:S(2)}) collective-permute-start(bf16[2,6,128,128]{3,2,1,0:T(8,128)(2,1)S(1)} %collective-permute-done.4.refs_10_), channel_id=1, source_target_pairs={{4,0},{0,4},{12,8},{8,12},{20,16},{16,20},{28,24},{24,28},{5,1},{1... | collective-permute-start | bytes 1179656 | tf_op jit(solution)/shard_map/ppermute | solution.py:189
  194.1 3.6 %collective-permute-start.26 = (bf16[2,6,128,128]{3,2,1,0:T(8,128)(2,1)}, bf16[2,6,128,128]{3,2,1,0:T(8,128)(2,1)S(1)}, u32[]{:S(2)}, u32[]{:S(2)}) collective-permute-start(bf16[2,6,128,128]{3,2,1,0:T(8,128)(2,1)} %collective-permute-done.22.refs_28_), channel_id=1, source_target_pairs={{4,0},{0,4},{12,8},{8,12},{20,16},{16,20},{28,24},{24,28},{5,1},{1... | collective-permute-start | bytes 1179656 | tf_op jit(solution)/shard_map/ppermute | solution.py:189
  195.6 6.6 %collective-permute-start.18 = (bf16[2,6,128,128]{3,2,1,0:T(8,128)(2,1)S(1)}, bf16[2,6,128,128]{3,2,1,0:T(8,128)(2,1)S(1)}, u32[]{:S(2)}, u32[]{:S(2)}) collective-permute-start(bf16[2,6,128,128]{3,2,1,0:T(8,128)(2,1)S(1)} %collective-permute-done.14.refs_20_), channel_id=1, source_target_pairs={{4,0},{0,4},{12,8},{8,12},{20,16},{16,20},{28,24},{24,28},{5,1},{1... | collective-permute-start | bytes 1179656 | tf_op jit(solution)/shard_map/ppermute | solution.py:189
  195.7 6.4 %collective-permute-start.10 = (bf16[2,6,128,128]{3,2,1,0:T(8,128)(2,1)}, bf16[2,6,128,128]{3,2,1,0:T(8,128)(2,1)}, u32[]{:S(2)}, u32[]{:S(2)}) collective-permute-start(bf16[2,6,128,128]{3,2,1,0:T(8,128)(2,1)} %copy-done.14), channel_id=1, source_target_pairs={{4,0},{0,4},{12,8},{8,12},{20,16},{16,20},{28,24},{24,28},{5,1},{1... | collective-permute-start | bytes 1179656 | tf_op jit(solution)/shard_map/ppermute | solution.py:189
  197.1 5.0 %collective-permute-start.25 = (bf16[2,6,128,128]{3,2,1,0:T(8,128)(2,1)}, bf16[2,6,128,128]{3,2,1,0:T(8,128)(2,1)}, u32[]{:S(2)}, u32[]{:S(2)}) collective-permute-start(bf16[2,6,128,128]{3,2,1,0:T(8,128)(2,1)} %copy-done.16), channel_id=1, source_target_pairs={{4,0},{0,4},{12,8},{8,12},{20,16},{16,20},{28,24},{24,28},{5,1},{1... | collective-permute-start | bytes 1179656 | tf_op jit(solution)/shard_map/ppermute | solution.py:189
  197.3 4.9 %collective-permute-start.17 = (bf16[2,6,128,128]{3,2,1,0:T(8,128)(2,1)}, bf16[2,6,128,128]{3,2,1,0:T(8,128)(2,1)}, u32[]{:S(2)}, u32[]{:S(2)}) collective-permute-start(bf16[2,6,128,128]{3,2,1,0:T(8,128)(2,1)} %copy-done.17), channel_id=1, source_target_pairs={{4,0},{0,4},{12,8},{8,12},{20,16},{16,20},{28,24},{24,28},{5,1},{1... | collective-permute-start | bytes 1179656 | tf_op jit(solution)/shard_map/ppermute | solution.py:189
  197.6 4.5 %collective-permute-start.9 = (bf16[2,6,128,128]{3,2,1,0:T(8,128)(2,1)}, bf16[2,6,128,128]{3,2,1,0:T(8,128)(2,1)}, u32[]{:S(2)}, u32[]{:S(2)}) collective-permute-start(bf16[2,6,128,128]{3,2,1,0:T(8,128)(2,1)} %copy-done.18), channel_id=1, source_target_pairs={{4,0},{0,4},{12,8},{8,12},{20,16},{16,20},{28,24},{24,28},{5,1},{1... | collective-permute-start | bytes 1179656 | tf_op jit(solution)/shard_map/ppermute | solution.py:189
  228.1 114.5 %reduce-scatter.5.cloned.1.call-start = ((), (), s32[]{:S(2)}) async-start(), calls=%async_computation.3 | async-start | bytes 3276800 | tf_op jit(solution)/shard_map/reduce_scatter | solution.py:206
  253.7 88.9 %copy-start.3 = (bf16[512,1280]{1,0:T(8,128)(2,1)S(1)}, bf16[512,1280]{1,0:T(8,128)(2,1)}, u32[]{:S(2)}) copy-start(bf16[512,1280]{1,0:T(8,128)(2,1)} %param.12) | copy-start | bytes 3932164
  (14 other events, 61.9 us)
Sparse Core Ops, SparseCore 0:
  9.0 35.3 all-gather.14
  46.0 31.6 all-gather.8
  79.3 31.6 all-gather.10
  112.5 31.6 all-gather.12
  228.2 60.3 reduce-scatter.2
  290.8 51.7 reduce-scatter.4

commit v2 on v1

v2 whole, which is shorter than its diff:
```python
import functools
import math

import jax
import jax.numpy as jnp
from jax import lax
from jax.experimental import pallas as pl
from jax.experimental.pallas import tpu as pltpu
from jax.sharding import PartitionSpec as P

HEAD_DIM = 128
EPSILON = 1e-06
NEG_FILL = -1e30
GATHER_PARTS = 4
QUERY_PARTS = 2
VMEM_BYTES = 56 * 1024 * 1024
FACTOR = math.log2(math.e) / math.sqrt(HEAD_DIM)


def gather_kernel(
    x_ref, shift_ref, scale_ref, wq_hbm, wk_hbm, wv_hbm, qg_ref, kg_ref,
    q_ref, kv_ref,
    w_ref, g_ref, normed_ref, own_ref,
    w_sem, right_send, right_recv, left_send, left_recv,
    peer_send, peer_recv, pair_send, pair_recv, local_sem,
):
    parts, shards, rows, width = g_ref.shape
    heads = q_ref.shape[1]
    model = shards * width
    spans = kv_ref.shape[0]
    pairs = spans // 2
    f, t = lax.axis_index("frame"), lax.axis_index("tensor")
    sibling = f + 1 - 2 * (f % 2)

    loads = [pltpu.make_async_copy(w, w_ref.at[i], w_sem.at[i]) for i, w in enumerate((wq_hbm, wk_hbm, wv_hbm))]
    for load in loads:
        load.start()

    barrier = pltpu.get_barrier_semaphore()

    def greet(device):
        pl.semaphore_signal(barrier, inc=1, device_id=device, device_id_type=pl.DeviceIdType.MESH)

    has_left, has_right = t > 0, t < shards - 1
    pl.when(has_left)(lambda: greet((f, t - 1)))
    pl.when(has_right)(lambda: greet((f, t + 1)))
    for k in range(1, pairs):
        greet(((f + 2 * k) % spans, t))
    greet((sibling, t))

    for c in range(parts):
        g_ref[c, t] = x_ref[c * rows : (c + 1) * rows]

    pl.semaphore_wait(barrier, pairs + jnp.where(has_left, 1, 0) + jnp.where(has_right, 1, 0))

    def remote(src, dst, send, recv, device):
        return pltpu.make_async_remote_copy(
            src_ref=src, dst_ref=dst, send_sem=send, recv_sem=recv,
            device_id=device, device_id_type=pl.DeviceIdType.MESH,
        )

    def go_right(c, d):
        block = g_ref.at[c, t - d]
        return remote(block, block, right_send.at[c, d], right_recv.at[c, d], (f, t + 1))

    def go_left(c, d):
        block = g_ref.at[c, t + d]
        return remote(block, block, left_send.at[c, d], left_recv.at[c, d], (f, t - 1))

    def come_right(c, d):
        block = g_ref.at[c, t - d]
        return remote(block, block, right_send.at[c, d - 1], right_recv.at[c, d - 1], (f, t - 1))

    def come_left(c, d):
        block = g_ref.at[c, t + d]
        return remote(block, block, left_send.at[c, d - 1], left_recv.at[c, d - 1], (f, t + 1))

    def to_peer(c, k):
        return remote(
            own_ref.at[c], kv_ref.at[2 * k, c], peer_send.at[c, k], peer_recv.at[c, k],
            ((f + spans - 2 * k) % spans, t),
        )

    def to_sibling(c, k):
        src = own_ref.at[c] if k == 0 else kv_ref.at[2 * k, c]
        return remote(src, kv_ref.at[2 * k + 1, c], pair_send.at[c, k], pair_recv.at[c, k], (sibling, t))

    def keep(c):
        return pltpu.make_async_copy(own_ref.at[c], kv_ref.at[0, c], local_sem.at[c])

    def send_own(c):
        pl.when(has_right)(lambda: go_right(c, 0).start())
        pl.when(has_left)(lambda: go_left(c, 0).start())

    def pass_on(c):
        for k in range(1, pairs):
            to_peer(c, k).wait_recv()
            to_sibling(c, k).start()

    ahead = min(2, parts)
    for c in range(ahead):
        send_own(c)

    def head_norm(shaped, gain):
        power = jnp.mean(shaped * shaped, axis=-1, keepdims=True)
        return (shaped * lax.rsqrt(power + EPSILON) * gain).astype(jnp.bfloat16)

    group = 2 if heads % 2 == 0 else 1
    span_width = group * HEAD_DIM

    def one_part(c, carried):
        for d in range(1, shards):

            @pl.when(t - d >= 0)
            def _():
                come_right(c, d).wait_recv()
                if d < shards - 1:
                    pl.when(has_right)(lambda: go_right(c, d).start())

            @pl.when(t + d < shards)
            def _():
                come_left(c, d).wait_recv()
                if d < shards - 1:
                    pl.when(has_left)(lambda: go_left(c, d).start())

        pl.when(c + ahead < parts)(lambda: send_own(c + ahead))

        total = jnp.zeros((rows, 1), jnp.float32)
        square = jnp.zeros((rows, 1), jnp.float32)
        for i in range(shards):
            x = g_ref[c, i].astype(jnp.float32)
            total += jnp.sum(x, axis=1, keepdims=True)
            square += jnp.sum(x * x, axis=1, keepdims=True)
        mean = total / model
        inverse = lax.rsqrt(square / model - mean * mean + EPSILON)
        for i in range(shards):
            columns = slice(i * width, (i + 1) * width)
            x = g_ref[c, i].astype(jnp.float32)
            y = (x - mean) * inverse * (1.0 + scale_ref[:, columns]) + shift_ref[:, columns]
            normed_ref[:, columns] = y.astype(jnp.bfloat16)

        @pl.when(c == 0)
        def _():
            for load in loads:
                load.wait()

        def one_group(j, carried):
            columns = pl.ds(pl.multiple_of(j * span_width, span_width), span_width)
            k, v, q = [
                jnp.dot(normed_ref[...], w_ref[i, :, columns], preferred_element_type=jnp.float32) for i in (1, 2, 0)
            ]
            for h in range(group):
                part = slice(h * HEAD_DIM, (h + 1) * HEAD_DIM)
                head = j * group + h
                own_ref[c, 0, head] = head_norm(k[:, part], kg_ref[head])
                own_ref[c, 1, head] = v[:, part].astype(jnp.bfloat16)
                q_ref[c, head] = head_norm(q[:, part], qg_ref[head])
            return carried

        lax.fori_loop(0, heads // group, one_group, 0)
        for k in range(1, pairs):
            to_peer(c, k).start()
        to_sibling(c, 0).start()
        keep(c).start()
        pl.when(c > 0)(lambda: pass_on(c - 1))
        return carried

    lax.fori_loop(0, parts, one_part, 0)
    pass_on(parts - 1)

    def finish(c, carried):
        for d in range(shards - 1):
            pl.when((t - d >= 0) & has_right)(lambda: go_right(c, d).wait_send())
            pl.when((t + d < shards) & has_left)(lambda: go_left(c, d).wait_send())
        for k in range(1, pairs):
            to_peer(c, k).wait_send()
        for k in range(pairs):
            to_sibling(c, k).wait()
        keep(c).wait()
        return carried

    lax.fori_loop(0, parts, finish, 0)


def gather_project(x, shift, scale, wq, wk, wv, qg, kg, parts):
    shards, spans = lax.axis_size("tensor"), lax.axis_size("frame")
    row_count, width = x.shape
    rows, model = row_count // parts, shards * width
    heads = wq.shape[1] // HEAD_DIM
    vmem = pl.BlockSpec(memory_space=pltpu.VMEM)
    hbm = pl.BlockSpec(memory_space=pl.ANY)
    dma = pltpu.SemaphoreType.DMA
    return pl.pallas_call(
        gather_kernel,
        in_specs=[vmem, vmem, vmem, hbm, hbm, hbm, vmem, vmem],
        out_specs=[vmem, hbm],
        out_shape=[
            jax.ShapeDtypeStruct((parts, heads, rows, HEAD_DIM), jnp.bfloat16),
            jax.ShapeDtypeStruct((spans, parts, 2, heads, rows, HEAD_DIM), jnp.bfloat16),
        ],
        scratch_shapes=[
            pltpu.VMEM((3, model, heads * HEAD_DIM), jnp.bfloat16),
            pltpu.VMEM((parts, shards, rows, width), jnp.bfloat16),
            pltpu.VMEM((rows, model), jnp.bfloat16),
            pltpu.VMEM((parts, 2, heads, rows, HEAD_DIM), jnp.bfloat16),
            dma((3,)),
        ]
        + [dma((parts, shards))] * 4
        + [dma((parts, spans // 2))] * 4
        + [dma((parts,))],
        compiler_params=pltpu.CompilerParams(vmem_limit_bytes=VMEM_BYTES, collective_id=0, has_side_effects=True),
        cost_estimate=pl.CostEstimate(
            flops=6 * row_count * model * heads * HEAD_DIM, bytes_accessed=6 * model * heads * HEAD_DIM, transcendentals=0
        ),
    )(x, shift, scale, wq, wk, wv, qg[:, None, :], kg[:, None, :])


def attend_kernel(live_ref, q_ref, kv_ref, o_ref, max_ref, sum_ref, acc_ref):
    sources, key_parts = kv_ref.shape[0], kv_ref.shape[1]
    q = jnp.concatenate([q_ref[i, 0] for i in range(q_ref.shape[0])], axis=0)
    block = kv_ref.shape[4] * key_parts

    def fold(s, first):
        live = live_ref[s]
        keys = jnp.concatenate([kv_ref[s, i, 0, 0] for i in range(key_parts)], axis=0)
        values = jnp.concatenate([kv_ref[s, i, 1, 0] for i in range(key_parts)], axis=0)
        scores = lax.dot_general(q, keys, (((1,), (1,)), ((), ())), preferred_element_type=jnp.float32)
        slot = lax.broadcasted_iota(jnp.int32, (1, block), 1)
        scores = jnp.where(slot < live, scores, NEG_FILL)
        top = jnp.max(scores, axis=1, keepdims=True)
        if not first:
            old = max_ref[:, :1]
            top = jnp.maximum(top, old)
            factor = jnp.exp2((old - top) * FACTOR)
        weights = jnp.exp2((scores - top) * FACTOR)
        total = weights[:, :HEAD_DIM]
        for i in range(1, block // HEAD_DIM):
            total += weights[:, i * HEAD_DIM : (i + 1) * HEAD_DIM]
        product = jnp.dot(weights.astype(jnp.bfloat16), values, preferred_element_type=jnp.float32)
        if first:
            sum_ref[...] = total
            acc_ref[...] = product
        else:
            sum_ref[...] = sum_ref[...] * factor + total
            acc_ref[...] = acc_ref[...] * factor + product
        max_ref[...] = jnp.broadcast_to(top, max_ref.shape)

    fold(0, True)
    for s in range(1, sources):
        pl.when(live_ref[s] > 0)(functools.partial(fold, s, False))
    o_ref[...] = (acc_ref[...] / jnp.sum(sum_ref[...], axis=1, keepdims=True)).astype(jnp.bfloat16)


def attend(live, queries, pieces, part, per):
    sources, key_parts, _, heads, part_rows, _ = pieces.shape
    rows = part_rows * per
    q_spec = pl.BlockSpec((per, 1, part_rows, HEAD_DIM), lambda h, live: (part, h, 0, 0))
    kv_spec = pl.BlockSpec((sources, key_parts, 2, 1, part_rows, HEAD_DIM), lambda h, live: (0, 0, 0, h, 0, 0))
    keys = sources * key_parts * part_rows
    return pl.pallas_call(
        attend_kernel,
        grid_spec=pltpu.PrefetchScalarGridSpec(
            num_scalar_prefetch=1,
            grid=(heads,),
            in_specs=[q_spec, kv_spec],
            out_specs=pl.BlockSpec((rows, HEAD_DIM), lambda h, live: (0, h)),
            scratch_shapes=[pltpu.VMEM((rows, HEAD_DIM), jnp.float32)] * 3,
        ),
        out_shape=jax.ShapeDtypeStruct((rows, heads * HEAD_DIM), jnp.bfloat16),
        compiler_params=pltpu.CompilerParams(vmem_limit_bytes=VMEM_BYTES),
        cost_estimate=pl.CostEstimate(
            flops=4 * rows * keys * heads * HEAD_DIM,
            bytes_accessed=4 * keys * heads * HEAD_DIM,
            transcendentals=rows * keys * heads,
        ),
    )(live, queries, pieces)


def on_device(
    latents,
    w_query,
    w_key,
    w_value,
    w_out,
    query_gain,
    key_gain,
    mod_table,
    levels,
    span_counts,
    block_mask,
    span_order,
):
    row_count, shard_width = latents.shape
    spans = lax.axis_size("frame")
    me = lax.axis_index("frame")
    column_start = lax.axis_index("tensor") * shard_width
    modulation = lax.dynamic_index_in_dim(mod_table, levels[0], 0, keepdims=False)
    shift_row, scale_row, gate_row = modulation[0:1], modulation[1:2], modulation[2]

    part_rows = row_count // GATHER_PARTS
    queries, pieces = gather_project(
        latents, shift_row, scale_row, w_query, w_key, w_value, query_gain, key_gain, GATHER_PARTS
    )

    offsets = jnp.arange(spans, dtype=jnp.int32)
    span_of = lax.rem(jnp.where(offsets % 2 == 0, me, me ^ 1) + offsets // 2 * 2, spans)
    own = offsets == 0
    allowed = (span_order[span_of] <= span_order[me]) & ((block_mask[0][span_of] == 1) | own)
    live = jnp.where(allowed, span_counts[span_of], 0).astype(jnp.int32)

    gate_part = lax.dynamic_slice_in_dim(gate_row, column_start, shard_width)
    per = GATHER_PARTS // QUERY_PARTS
    results = []
    for c in range(QUERY_PARTS):
        attended = attend(live, queries, pieces, c, per)
        partial_out = jnp.dot(attended, w_out, preferred_element_type=jnp.float32).astype(jnp.bfloat16)
        projected = lax.psum_scatter(partial_out, "tensor", scatter_dimension=1, tiled=True).astype(jnp.float32)
        rows = latents[c * per * part_rows : (c + 1) * per * part_rows].astype(jnp.float32)
        results.append((rows + gate_part * projected).astype(jnp.bfloat16))
    return jnp.concatenate(results, axis=0)


def solution(mesh):
    return jax.shard_map(
        on_device,
        mesh=mesh,
        in_specs=(
            P("frame", "tensor"),
            P(None, "tensor"),
            P(None, "tensor"),
            P(None, "tensor"),
            P("tensor", None),
            P("tensor", None),
            P("tensor", None),
            P(),
            P("frame"),
            P(),
            P("frame", None),
            P(),
        ),
        out_specs=P("frame", "tensor"),
        check_vma=False,
    )
```

time: 355 us -> 286 us (0.81)
  waiting for transfers between devices: 204 us -> 96.7 us
  Pallas kernels: 85.6 us -> 145 us
  starting transfers between devices: 18.7 us -> 0.22 us
    all_gather x4 -> x0, waiting for transfers between devices: 83.7 us -> none  [on_device(): x = lax.all_gather(block, 'tensor', axis=0)]
    pallas_call x6 -> x3, Pallas kernels: 85.6 us -> 145 us  [the longest x1 122 us: gather_project(): pl.pallas_call(gather_kernel, in_specs=[vmem, vmem, vmem, hbm, hbm, hbm,...]
    ppermute x28 -> x0, waiting for transfers between devices: 30.5 us -> none  [the longest x12 29.4 us: from_ahead(): lax.ppermute(block, 'frame', [((i + distance) % spans, i) for i in range(...]
    ppermute x28 -> x0, starting transfers between devices: 18.3 us -> none  [the longest x12 15.4 us: from_ahead(): lax.ppermute(block, 'frame', [((i + distance) % spans, i) for i in range(...]
    reduce_scatter x2, waiting for transfers between devices: 87.9 us -> 96.7 us  [on_device(): lax.psum_scatter(partial_out, 'tensor', scatter_dimension=1, tiled=True)]
  transfers between devices with their start and end apart: 34 -> 2, of which waited for: 12 -> 2; matrix products, arithmetic and copies ran while one was open for 5% -> 3% of each run, Pallas kernels for 19% -> 4%
where the time goes in v2:
time: 286 us; the launch traced here: 284 us
  Pallas kernels  145 us (51%)
  waiting for transfers between devices  96.7 us (34%)
  matrix products  14.1 us (5%)
  between operations  14.1 us (5%)
  local copies, waits for them, and re-layouts  10.7 us (4%)
  other arithmetic  2.91 us (1%)
    pallas_call x1, Pallas kernels, gather_project(): pl.pallas_call(gather_kernel, in_specs=[vmem, vmem, vmem, hbm, hbm, hbm,...  122 us
    reduce_scatter x2, waiting for transfers between devices, on_device(): lax.psum_scatter(partial_out, 'tensor', scatter_dimension=1, tiled=True)  96.7 us
    pallas_call x2, Pallas kernels, attend(): pl.pallas_call(attend_kernel, grid_spec=pltpu.PrefetchScalarGridSpec(num_...  22.4 us
    dot_general x2, matrix products, on_device(): jnp.dot(attended, w_out, preferred_element_type=jnp.float32)  14.1 us
  transfers between devices with their start and end apart: 2, of which 2 were waited for; matrix products, arithmetic and copies ran while one was open for 3% of the time, Pallas kernels for 4%

profile of v2, /device:TPU:0, one launch (start us, length us, event | category | flops | bytes accessed | tf_op | source)
XLA Modules:
  0.0 283.6 jit_solution(2601948718281958510)
XLA Ops:
  6.5 0.0 copy-start
  6.5 0.0 reduce-scatter.3.cloned.1.call-start
  7.2 1.3 broadcast_in_dim.23.qg_ref
  8.5 1.3 broadcast_in_dim.24.kg_ref
  9.8 1.3 dynamic_slice.12
  11.1 1.3 gather_fusion
  12.4 1.3 gather_fusion.2
  13.7 0.0 copy-done
  13.7 0.6 gather_fusion.1
  14.3 1.6 dynamic-slice_bitcast_fusion
  16.0 1.2 and_select_fusion.live_ref
  17.2 122.4 %shard_map.118 = (bf16[4,6,128,128]{3,2,1,0:T(8,128)(2,1)}, bf16[8,4,2,6,128,128]{5,4,3,2,1,0:T(8,128)(2,1)}) custom-call(bf16[512,1280]{1,0:T(8,128)(2,1)} %x_ref.1, f32[1,5120]{1,0:T(1,128)} %get-tuple-element.12.shift_ref, f32[1,5120]{1,0:T(1,128)} %get-tuple-element.11.scale_ref, bf16[5120,768]{1,0:T(8,128)(2,1)} %wq_hbm.1, bf16[5120,768]{1,0:T(8,128)(2,1)} %wk_hbm.1, ...), custom_call_target="tpu_custom_call" | custom-call | flops 12079595520 | bytes 23592960 | tf_op jit(solution)/shard_map/pallas_call | solution.py:193
  139.5 11.2 %shard_map.119 = bf16[256,768]{1,0:T(8,128)(2,1)} custom-call(s32[8]{0:T(128)} %and_select_fusion.live_ref, bf16[4,6,128,128]{3,2,1,0:T(8,128)(2,1)} %get-tuple-element.7.q_ref, bf16[8,4,2,6,128,128]{5,4,3,2,1,0:T(8,128)(2,1)} %get-tuple-element.8.kv_ref), custom_call_target="tpu_custom_call" | custom-call | flops 3221225472 | bytes 12582912 | tf_op jit(solution)/shard_map/pallas_call | solution.py:260
  150.7 7.1 %convolution_convert_fusion.1 = bf16[256,5120]{1,0:T(8,128)(2,1)} fusion(bf16[256,768]{1,0:T(8,128)(2,1)} %shard_map.119, bf16[768,5120]{1,0:T(8,128)(2,1)} %param.16), kind=kOutput, calls=%fused_computation.4 | convolution fusion | flops 2014576640 | bytes 10878976 | tf_op jit(solution)/shard_map/dot_general | solution.py:316
  157.8 0.0 reduce-scatter.3.cloned.1.call-update
  157.8 0.2 reduce-scatter.5.cloned.1.call-start
  158.0 11.2 %shard_map.120 = bf16[256,768]{1,0:T(8,128)(2,1)} custom-call(s32[8]{0:T(128)} %and_select_fusion.live_ref, bf16[4,6,128,128]{3,2,1,0:T(8,128)(2,1)} %get-tuple-element.7.q_ref, bf16[8,4,2,6,128,128]{5,4,3,2,1,0:T(8,128)(2,1)} %get-tuple-element.8.kv_ref), custom_call_target="tpu_custom_call" | custom-call | flops 3221225472 | bytes 12582912 | tf_op jit(solution)/shard_map/pallas_call | solution.py:260
  169.2 7.1 %convolution_convert_fusion = bf16[256,5120]{1,0:T(8,128)(2,1)} fusion(bf16[256,768]{1,0:T(8,128)(2,1)} %shard_map.120, bf16[768,5120]{1,0:T(8,128)(2,1)} %param.16), kind=kOutput, calls=%fused_computation.3 | convolution fusion | flops 2014576640 | bytes 10878976 | tf_op jit(solution)/shard_map/dot_general | solution.py:316
  176.3 0.0 copy-start.1
  176.3 0.0 reduce-scatter.5.cloned.1.call-update
  176.4 1.0 dynamic-slice_reduce_fusion
  177.3 42.6 %reduce-scatter.3.cloned.1.call-done = bf16[256,1280]{1,0:T(8,128)(2,1)} async-done(((bf16[256,5120]{1,0:T(8,128)(2,1)}), bf16[256,1280]{1,0:T(8,128)(2,1)}) %reduce-scatter.3.cloned.1.call-update) | async-done | bytes 655376 | tf_op jit(solution)/shard_map/reduce_scatter | solution.py:317
  219.9 54.1 %reduce-scatter.5.cloned.1.call-done = bf16[256,1280]{1,0:T(8,128)(2,1)} async-done(((bf16[256,5120]{1,0:T(8,128)(2,1)}), bf16[256,1280]{1,0:T(8,128)(2,1)}) %reduce-scatter.5.cloned.1.call-update) | async-done | bytes 655376 | tf_op jit(solution)/shard_map/reduce_scatter | solution.py:317
  274.0 0.0 copy-done.1
  274.0 1.7 add_convert_fusion.1
  275.7 0.0 copy-start.2
  275.7 1.0 copy-done.2
  (3 shorter events, 0.0 us)
Async XLA Ops:
  6.5 7.1 %copy-start = (s32[1,8]{1,0:T(1,128)S(1)}, s32[1,8]{1,0:T(1,128)}, u32[]{:S(2)}) copy-start(s32[1,8]{1,0:T(1,128)} %param.22) | copy-start | bytes 100
  6.5 213.4 %reduce-scatter.3.cloned.1.call-start = ((), (), s32[]{:S(2)}) async-start(), calls=%async_computation.2 | async-start | bytes 3276800 | tf_op jit(solution)/shard_map/reduce_scatter | solution.py:317
  157.8 116.2 %reduce-scatter.5.cloned.1.call-start = ((), (), s32[]{:S(2)}) async-start(), calls=%async_computation.3 | async-start | bytes 3276800 | tf_op jit(solution)/shard_map/reduce_scatter | solution.py:317
  176.3 97.7 %copy-start.1 = (bf16[512,1280]{1,0:T(8,128)(2,1)S(1)}, bf16[512,1280]{1,0:T(8,128)(2,1)}, u32[]{:S(2)}) copy-start(bf16[512,1280]{1,0:T(8,128)(2,1)} %x_ref.1) | copy-start | bytes 3932164
  275.7 1.1 copy-start.2
Sparse Core Ops, SparseCore 0:
  157.9 61.9 reduce-scatter.2
  222.2 51.7 reduce-scatter.4

commit v3 on v2

--- a/solution.py
+++ b/solution.py
@@ -1,4 +1,3 @@
-import functools
 import math
 
 import jax
@@ -12,7 +11,6 @@
 EPSILON = 1e-06
 NEG_FILL = -1e30
 GATHER_PARTS = 4
-QUERY_PARTS = 2
 VMEM_BYTES = 56 * 1024 * 1024
 FACTOR = math.log2(math.e) / math.sqrt(HEAD_DIM)
 
@@ -215,65 +213,169 @@
     )(x, shift, scale, wq, wk, wv, qg[:, None, :], kg[:, None, :])
 
 
-def attend_kernel(live_ref, q_ref, kv_ref, o_ref, max_ref, sum_ref, acc_ref):
-    sources, key_parts = kv_ref.shape[0], kv_ref.shape[1]
-    q = jnp.concatenate([q_ref[i, 0] for i in range(q_ref.shape[0])], axis=0)
-    block = kv_ref.shape[4] * key_parts
-
-    def fold(s, first):
-        live = live_ref[s]
-        keys = jnp.concatenate([kv_ref[s, i, 0, 0] for i in range(key_parts)], axis=0)
-        values = jnp.concatenate([kv_ref[s, i, 1, 0] for i in range(key_parts)], axis=0)
-        scores = lax.dot_general(q, keys, (((1,), (1,)), ((), ())), preferred_element_type=jnp.float32)
-        slot = lax.broadcasted_iota(jnp.int32, (1, block), 1)
-        scores = jnp.where(slot < live, scores, NEG_FILL)
-        top = jnp.max(scores, axis=1, keepdims=True)
-        if not first:
-            old = max_ref[:, :1]
-            top = jnp.maximum(top, old)
-            factor = jnp.exp2((old - top) * FACTOR)
-        weights = jnp.exp2((scores - top) * FACTOR)
-        total = weights[:, :HEAD_DIM]
-        for i in range(1, block // HEAD_DIM):
-            total += weights[:, i * HEAD_DIM : (i + 1) * HEAD_DIM]
-        product = jnp.dot(weights.astype(jnp.bfloat16), values, preferred_element_type=jnp.float32)
-        if first:
-            sum_ref[...] = total
-            acc_ref[...] = product
-        else:
-            sum_ref[...] = sum_ref[...] * factor + total
-            acc_ref[...] = acc_ref[...] * factor + product
-        max_ref[...] = jnp.broadcast_to(top, max_ref.shape)
-
-    fold(0, True)
-    for s in range(1, sources):
-        pl.when(live_ref[s] > 0)(functools.partial(fold, s, False))
-    o_ref[...] = (acc_ref[...] / jnp.sum(sum_ref[...], axis=1, keepdims=True)).astype(jnp.bfloat16)
-
-
-def attend(live, queries, pieces, part, per):
-    sources, key_parts, _, heads, part_rows, _ = pieces.shape
-    rows = part_rows * per
-    q_spec = pl.BlockSpec((per, 1, part_rows, HEAD_DIM), lambda h, live: (part, h, 0, 0))
-    kv_spec = pl.BlockSpec((sources, key_parts, 2, 1, part_rows, HEAD_DIM), lambda h, live: (0, 0, 0, h, 0, 0))
-    keys = sources * key_parts * part_rows
+def attend_kernel(
+    live_ref, q_ref, kv_hbm, wo_hbm, x_ref, gate_ref,
+    o_ref,
+    kv_ref, wo_ref, attended_ref, part_ref, right_ref, left_ref, total_ref,
+    kv_sem, wo_sem, right_send, right_recv, left_send, left_recv,
+):
+    heads, sources, parts, _, rows, _ = kv_ref.shape
+    shards, width = part_ref.shape[1], part_ref.shape[3]
+    block = parts * rows
+    f, t = lax.axis_index("frame"), lax.axis_index("tensor")
+    has_left, has_right = t > 0, t < shards - 1
+
+    def load(h):
+        return pltpu.make_async_copy(kv_hbm.at[:, :, :, h], kv_ref.at[h], kv_sem.at[h])
+
+    for h in range(heads):
+        load(h).start()
+    load_out = pltpu.make_async_copy(wo_hbm, wo_ref, wo_sem)
+    load_out.start()
+
+    barrier = pltpu.get_barrier_semaphore()
+
+    def greet(device):
+        pl.semaphore_signal(barrier, inc=1, device_id=device, device_id_type=pl.DeviceIdType.MESH)
+
+    pl.when(has_left)(lambda: greet((f, t - 1)))
+    pl.when(has_right)(lambda: greet((f, t + 1)))
+    pl.semaphore_wait(barrier, jnp.where(has_left, 1, 0) + jnp.where(has_right, 1, 0))
+
+    def right(c, j, src):
+        return pltpu.make_async_remote_copy(
+            src_ref=src.at[c, j], dst_ref=right_ref.at[c, j], send_sem=right_send.at[c, j], recv_sem=right_recv.at[c, j],
+            device_id=(f, t + 1), device_id_type=pl.DeviceIdType.MESH,
+        )
+
+    def left(c, j, src):
+        return pltpu.make_async_remote_copy(
+            src_ref=src.at[c, j], dst_ref=left_ref.at[c, j], send_sem=left_send.at[c, j], recv_sem=left_recv.at[c, j],
+            device_id=(f, t - 1), device_id_type=pl.DeviceIdType.MESH,
+        )
+
+    def begin(c):
+        @pl.when(t == 0)
+        def _():
+            for j in range(shards - 1, 0, -1):
+                right(c, j, part_ref).start()
+
+        @pl.when(t == shards - 1)
+        def _():
+            for j in range(shards - 1):
+                left(c, j, part_ref).start()
+
+    def relay(c):
+        for e in range(shards - 1, 0, -1):
+
+            @pl.when(has_left & (t + e < shards))
+            def _():
+                j = t + e
+                right(c, j, right_ref).wait_recv()
+                both = right_ref[c, j].astype(jnp.float32) + part_ref[c, j].astype(jnp.float32)
+                right_ref[c, j] = both.astype(jnp.bfloat16)
+                right(c, j, right_ref).start()
+
+            @pl.when(has_right & (t - e >= 0))
+            def _():
+                j = t - e
+                left(c, j, left_ref).wait_recv()
+                both = left_ref[c, j].astype(jnp.float32) + part_ref[c, j].astype(jnp.float32)
+                left_ref[c, j] = both.astype(jnp.bfloat16)
+                left(c, j, left_ref).start()
+
+    def one_part(c, carried):
+        def one_head(h, carried):
+            pl.when(c == 0)(lambda: load(h).wait())
+            q = q_ref[c, h]
+            for s in range(sources):
+                keys = jnp.concatenate([kv_ref[h, s, i, 0] for i in range(parts)], axis=0)
+                values = jnp.concatenate([kv_ref[h, s, i, 1] for i in range(parts)], axis=0)
+                scores = lax.dot_general(q, keys, (((1,), (1,)), ((), ())), preferred_element_type=jnp.float32)
+                slot = lax.broadcasted_iota(jnp.int32, (1, block), 1)
+                scores = jnp.where(slot < live_ref[s], scores, NEG_FILL)
+                top = jnp.max(scores, axis=1, keepdims=True)
+                if s > 0:
+                    top = jnp.maximum(top, best)
+                    factor = jnp.exp2((best - top) * FACTOR)
+                best = top
+                weights = jnp.exp2((scores - top) * FACTOR)
+                total = weights[:, :HEAD_DIM]
+                for i in range(1, block // HEAD_DIM):
+                    total += weights[:, i * HEAD_DIM : (i + 1) * HEAD_DIM]
+                product = jnp.dot(weights.astype(jnp.bfloat16), values, preferred_element_type=jnp.float32)
+                if s == 0:
+                    summed, accum = total, product
+                else:
+                    summed, accum = summed * factor + total, accum * factor + product
+            result = accum / jnp.sum(summed, axis=1, keepdims=True)
+            attended_ref[h] = result.astype(jnp.bfloat16)
+            return carried
+
+        lax.fori_loop(0, heads, one_head, 0)
+        pl.when(c == 0)(lambda: load_out.wait())
+        attended = jnp.concatenate([attended_ref[h] for h in range(heads)], axis=1)
+        for j in range(shards):
+            term = jnp.dot(attended, wo_ref[:, j * width : (j + 1) * width], preferred_element_type=jnp.float32)
+            part_ref[c, j] = term.astype(jnp.bfloat16)
+        begin(c)
+        pl.when(c > 0)(lambda: relay(c - 1))
+        return carried
+
+    lax.fori_loop(0, parts, one_part, 0)
+    relay(parts - 1)
+
+    def finish(c, carried):
+        total_ref[...] = part_ref[c, t].astype(jnp.float32)
+
+        @pl.when(has_left)
+        def _():
+            right(c, t, right_ref).wait_recv()
+            total_ref[...] += right_ref[c, t].astype(jnp.float32)
+
+        @pl.when(has_right)
+        def _():
+            left(c, t, left_ref).wait_recv()
+            total_ref[...] += left_ref[c, t].astype(jnp.float32)
+
+        here = pl.ds(pl.multiple_of(c * rows, rows), rows)
+        updated = x_ref[here, :].astype(jnp.float32) + gate_ref[...] * total_ref[...]
+        o_ref[here, :] = updated.astype(jnp.bfloat16)
+        for e in range(1, shards):
+            pl.when(t + e < shards)(lambda: right(c, t + e, right_ref).wait_send())
+            pl.when(t - e >= 0)(lambda: left(c, t - e, left_ref).wait_send())
+        return carried
+
+    lax.fori_loop(0, parts, finish, 0)
+
+
+def attend_project(live, queries, pieces, wo, x, gate):
+    sources, parts, _, heads, rows, _ = pieces.shape
+    shards, width = lax.axis_size("tensor"), x.shape[1]
+    vmem = pl.BlockSpec(memory_space=pltpu.VMEM)
+    hbm = pl.BlockSpec(memory_space=pl.ANY)
+    dma = pltpu.SemaphoreType.DMA
+    keys = sources * parts * rows
     return pl.pallas_call(
         attend_kernel,
-        grid_spec=pltpu.PrefetchScalarGridSpec(
-            num_scalar_prefetch=1,
-            grid=(heads,),
-            in_specs=[q_spec, kv_spec],
-            out_specs=pl.BlockSpec((rows, HEAD_DIM), lambda h, live: (0, h)),
-            scratch_shapes=[pltpu.VMEM((rows, HEAD_DIM), jnp.float32)] * 3,
+        in_specs=[pl.BlockSpec(memory_space=pltpu.SMEM), vmem, hbm, hbm, vmem, vmem],
+        out_specs=vmem,
+        out_shape=jax.ShapeDtypeStruct(x.shape, jnp.bfloat16),
+        scratch_shapes=[
+            pltpu.VMEM((heads, sources, parts, 2, rows, HEAD_DIM), jnp.bfloat16),
+            pltpu.VMEM(wo.shape, jnp.bfloat16),
+            pltpu.VMEM((heads, rows, HEAD_DIM), jnp.bfloat16),
+        ]
+        + [pltpu.VMEM((parts, shards, rows, width), jnp.bfloat16)] * 3
+        + [pltpu.VMEM((rows, width), jnp.float32), dma((heads,)), dma]
+        + [dma((parts, shards))] * 4,
+        compiler_params=pltpu.CompilerParams(vmem_limit_bytes=VMEM_BYTES, collective_id=1, has_side_effects=True),
+        cost_estimate=pl.CostEstimate(
+            flops=4 * x.shape[0] * keys * heads * HEAD_DIM,
+            bytes_accessed=4 * keys * heads * HEAD_DIM,
+            transcendentals=x.shape[0] * keys * heads,
         ),
-        out_shape=jax.ShapeDtypeStruct((rows, heads * HEAD_DIM), jnp.bfloat16),
-        compiler_params=pltpu.CompilerParams(vmem_limit_bytes=VMEM_BYTES),
-        cost_estimate=pl.CostEstimate(
-            flops=4 * rows * keys * heads * HEAD_DIM,
-            bytes_accessed=4 * keys * heads * HEAD_DIM,
-            transcendentals=rows * keys * heads,
-        ),
-    )(live, queries, pieces)
+    )(live, queries, pieces, wo, x, gate)
 
 
 def on_device(
@@ -290,14 +392,13 @@
     block_mask,
     span_order,
 ):
-    row_count, shard_width = latents.shape
+    shard_width = latents.shape[1]
     spans = lax.axis_size("frame")
     me = lax.axis_index("frame")
     column_start = lax.axis_index("tensor") * shard_width
     modulation = lax.dynamic_index_in_dim(mod_table, levels[0], 0, keepdims=False)
-    shift_row, scale_row, gate_row = modulation[0:1], modulation[1:2], modulation[2]
-
-    part_rows = row_count // GATHER_PARTS
+    shift_row, scale_row, gate_row = modulation[0:1], modulation[1:2], modulation[2:3]
+
     queries, pieces = gather_project(
         latents, shift_row, scale_row, w_query, w_key, w_value, query_gain, key_gain, GATHER_PARTS
     )
@@ -308,16 +409,8 @@
     allowed = (span_order[span_of] <= span_order[me]) & ((block_mask[0][span_of] == 1) | own)
     live = jnp.where(allowed, span_counts[span_of], 0).astype(jnp.int32)
 
-    gate_part = lax.dynamic_slice_in_dim(gate_row, column_start, shard_width)
-    per = GATHER_PARTS // QUERY_PARTS
-    results = []
-    for c in range(QUERY_PARTS):
-        attended = attend(live, queries, pieces, c, per)
-        partial_out = jnp.dot(attended, w_out, preferred_element_type=jnp.float32).astype(jnp.bfloat16)
-        projected = lax.psum_scatter(partial_out, "tensor", scatter_dimension=1, tiled=True).astype(jnp.float32)
-        rows = latents[c * per * part_rows : (c + 1) * per * part_rows].astype(jnp.float32)
-        results.append((rows + gate_part * projected).astype(jnp.bfloat16))
-    return jnp.concatenate(results, axis=0)
+    gate_part = lax.dynamic_slice_in_dim(gate_row, column_start, shard_width, axis=1)
+    return attend_project(live, queries, pieces, w_out, latents, gate_part)
 
 
 def solution(mesh):

time: 286 us -> 248 us (0.87)
  waiting for transfers between devices: 96.7 us -> 0 us
  Pallas kernels: 145 us -> 233 us
  matrix products: 14.1 us -> 0 us
  between operations: 14.1 us -> 0.7 us
    reduce_scatter x2 -> x0, waiting for transfers between devices: 96.7 us -> none  [on_device(): lax.psum_scatter(partial_out, 'tensor', scatter_dimension=1, tiled=True)]
    pallas_call x2 -> x1, Pallas kernels: 22.4 us -> 111 us  [attend_project(): pl.pallas_call(attend_kernel, in_specs=[pl.BlockSpec(memory_space=pltpu.S...]
    dot_general x2 -> x0, matrix products: 14.1 us -> none  [on_device(): jnp.dot(attended, w_out, preferred_element_type=jnp.float32)]
  transfers between devices with their start and end apart: 2 -> 0, of which waited for: 2 -> 0; matrix products, arithmetic and copies ran while one was open for 3% -> 0% of each run, Pallas kernels for 4% -> 0%
where the time goes in v3:
time: 248 us
  Pallas kernels  233 us (94%)
  local copies, waits for them, and re-layouts  12.6 us (5%)
    pallas_call x1, Pallas kernels, gather_project(): pl.pallas_call(gather_kernel, in_specs=[vmem, vmem, vmem, hbm, hbm, hbm,...  122 us
    pallas_call x1, Pallas kernels, attend_project(): pl.pallas_call(attend_kernel, in_specs=[pl.BlockSpec(memory_space=pltpu.S...  111 us

profile of v3, /device:TPU:0, one launch (start us, length us, event | category | flops | bytes accessed | tf_op | source)
XLA Modules:
  0.0 247.9 jit_solution(16441347418916262689)
XLA Ops:
  0.0 0.0 copy-start
  0.7 1.2 dynamic_slice.12
  1.9 0.0 copy-done
  1.9 1.3 broadcast_in_dim.21.qg_ref
  3.2 1.3 broadcast_in_dim.22.kg_ref
  4.5 1.3 gather_fusion.2
  5.8 0.6 gather_fusion.1
  6.5 1.3 gather_fusion
  7.8 1.2 and_select_fusion.live_ref
  9.0 1.5 dynamic-slice_bitcast_fusion.2.gate_ref
  10.5 1.6 dynamic-slice_bitcast_fusion
  12.1 122.3 %shard_map.118 = (bf16[4,6,128,128]{3,2,1,0:T(8,128)(2,1)}, bf16[8,4,2,6,128,128]{5,4,3,2,1,0:T(8,128)(2,1)}) custom-call(bf16[512,1280]{1,0:T(8,128)(2,1)} %x_ref.3, f32[1,5120]{1,0:T(1,128)} %get-tuple-element.10.shift_ref, f32[1,5120]{1,0:T(1,128)} %get-tuple-element.9.scale_ref, bf16[5120,768]{1,0:T(8,128)(2,1)} %wq_hbm.1, bf16[5120,768]{1,0:T(8,128)(2,1)} %wk_hbm.1, ...), custom_call_target="tpu_custom_call" | custom-call | flops 12079595520 | bytes 23592960 | tf_op jit(solution)/shard_map/pallas_call | solution.py:191
  134.4 111.0 %shard_map.119 = bf16[512,1280]{1,0:T(8,128)(2,1)} custom-call(s32[8]{0:T(128)} %and_select_fusion.live_ref, bf16[4,6,128,128]{3,2,1,0:T(8,128)(2,1)} %get-tuple-element.7.q_ref, bf16[8,4,2,6,128,128]{5,4,3,2,1,0:T(8,128)(2,1)} %get-tuple-element.8.kv_hbm, bf16[768,5120]{1,0:T(8,128)(2,1)} %wo_hbm.1, bf16[512,1280]{1,0:T(8,128)(2,1)} %x_ref.3, ...), custom_call_target="tpu_custom_call" | custom-call | flops 6442450944 | bytes 12582912 | tf_op jit(solution)/shard_map/pallas_call | solution.py:359
  245.4 2.5 copy.15
  (2 shorter events, 0.0 us)
Async XLA Ops:
  0.0 1.9 copy-start

commit v4 on v3

--- a/solution.py
+++ b/solution.py
@@ -16,7 +16,7 @@
 
 
 def gather_kernel(
-    x_ref, shift_ref, scale_ref, wq_hbm, wk_hbm, wv_hbm, qg_ref, kg_ref,
+    level_ref, x_ref, mod_ref, wq_hbm, wk_hbm, wv_hbm, qg_ref, kg_ref,
     q_ref, kv_ref,
     w_ref, g_ref, normed_ref, own_ref,
     w_sem, right_send, right_recv, left_send, left_recv,
@@ -26,6 +26,7 @@
     heads = q_ref.shape[1]
     model = shards * width
     spans = kv_ref.shape[0]
+    level = level_ref[0]
     pairs = spans // 2
     f, t = lax.axis_index("frame"), lax.axis_index("tensor")
     sibling = f + 1 - 2 * (f % 2)
@@ -134,7 +135,7 @@
         for i in range(shards):
             columns = slice(i * width, (i + 1) * width)
             x = g_ref[c, i].astype(jnp.float32)
-            y = (x - mean) * inverse * (1.0 + scale_ref[:, columns]) + shift_ref[:, columns]
+            y = (x - mean) * inverse * (1.0 + mod_ref[1, pl.ds(level, 1), columns]) + mod_ref[0, pl.ds(level, 1), columns]
             normed_ref[:, columns] = y.astype(jnp.bfloat16)
 
         @pl.when(c == 0)
@@ -142,24 +143,33 @@
             for load in loads:
                 load.wait()
 
-        def one_group(j, carried):
+        def product(i, j):
             columns = pl.ds(pl.multiple_of(j * span_width, span_width), span_width)
-            k, v, q = [
-                jnp.dot(normed_ref[...], w_ref[i, :, columns], preferred_element_type=jnp.float32) for i in (1, 2, 0)
-            ]
+            return jnp.dot(normed_ref[...], w_ref[i, :, columns], preferred_element_type=jnp.float32)
+
+        def keys_values(j, carried):
+            k, v = product(1, j), product(2, j)
             for h in range(group):
                 part = slice(h * HEAD_DIM, (h + 1) * HEAD_DIM)
                 head = j * group + h
-                own_ref[c, 0, head] = head_norm(k[:, part], kg_ref[head])
+                own_ref[c, 0, head] = head_norm(k[:, part], kg_ref[pl.ds(head, 1), :])
                 own_ref[c, 1, head] = v[:, part].astype(jnp.bfloat16)
-                q_ref[c, head] = head_norm(q[:, part], qg_ref[head])
             return carried
 
-        lax.fori_loop(0, heads // group, one_group, 0)
+        def queries(j, carried):
+            q = product(0, j)
+            for h in range(group):
+                part = slice(h * HEAD_DIM, (h + 1) * HEAD_DIM)
+                head = j * group + h
+                q_ref[c, head] = head_norm(q[:, part], qg_ref[pl.ds(head, 1), :])
+            return carried
+
+        lax.fori_loop(0, heads // group, keys_values, 0)
         for k in range(1, pairs):
             to_peer(c, k).start()
         to_sibling(c, 0).start()
         keep(c).start()
+        lax.fori_loop(0, heads // group, queries, 0)
         pl.when(c > 0)(lambda: pass_on(c - 1))
         return carried
 
@@ -180,7 +190,7 @@
     lax.fori_loop(0, parts, finish, 0)
 
 
-def gather_project(x, shift, scale, wq, wk, wv, qg, kg, parts):
+def gather_project(level, x, mod, wq, wk, wv, qg, kg, parts):
     shards, spans = lax.axis_size("tensor"), lax.axis_size("frame")
     row_count, width = x.shape
     rows, model = row_count // parts, shards * width
@@ -190,7 +200,7 @@
     dma = pltpu.SemaphoreType.DMA
     return pl.pallas_call(
         gather_kernel,
-        in_specs=[vmem, vmem, vmem, hbm, hbm, hbm, vmem, vmem],
+        in_specs=[pl.BlockSpec(memory_space=pltpu.SMEM), vmem, vmem, hbm, hbm, hbm, vmem, vmem],
         out_specs=[vmem, hbm],
         out_shape=[
             jax.ShapeDtypeStruct((parts, heads, rows, HEAD_DIM), jnp.bfloat16),
@@ -210,11 +220,11 @@
         cost_estimate=pl.CostEstimate(
             flops=6 * row_count * model * heads * HEAD_DIM, bytes_accessed=6 * model * heads * HEAD_DIM, transcendentals=0
         ),
-    )(x, shift, scale, wq, wk, wv, qg[:, None, :], kg[:, None, :])
+    )(level, x, mod, wq, wk, wv, qg, kg)
 
 
 def attend_kernel(
-    live_ref, q_ref, kv_hbm, wo_hbm, x_ref, gate_ref,
+    level_ref, counts_ref, mask_ref, order_ref, q_ref, kv_hbm, wo_hbm, x_ref, mod_ref,
     o_ref,
     kv_ref, wo_ref, attended_ref, part_ref, right_ref, left_ref, total_ref,
     kv_sem, wo_sem, right_send, right_recv, left_send, left_recv,
@@ -225,6 +235,15 @@
     f, t = lax.axis_index("frame"), lax.axis_index("tensor")
     has_left, has_right = t > 0, t < shards - 1
 
+    live = []
+    for s in range(sources):
+        base = f if s % 2 == 0 else f + 1 - 2 * (f % 2)
+        span = (base + s // 2 * 2) % sources
+        allowed = order_ref[span] <= order_ref[f]
+        if s > 0:
+            allowed = allowed & (mask_ref[0, span] == 1)
+        live.append(jnp.where(allowed, counts_ref[span], 0))
+
     def load(h):
         return pltpu.make_async_copy(kv_hbm.at[:, :, :, h], kv_ref.at[h], kv_sem.at[h])
 
@@ -293,7 +312,7 @@
                 values = jnp.concatenate([kv_ref[h, s, i, 1] for i in range(parts)], axis=0)
                 scores = lax.dot_general(q, keys, (((1,), (1,)), ((), ())), preferred_element_type=jnp.float32)
                 slot = lax.broadcasted_iota(jnp.int32, (1, block), 1)
-                scores = jnp.where(slot < live_ref[s], scores, NEG_FILL)
+                scores = jnp.where(slot < live[s], scores, NEG_FILL)
                 top = jnp.max(scores, axis=1, keepdims=True)
                 if s > 0:
                     top = jnp.maximum(top, best)
@@ -339,7 +358,8 @@
             total_ref[...] += left_ref[c, t].astype(jnp.float32)
 
         here = pl.ds(pl.multiple_of(c * rows, rows), rows)
-        updated = x_ref[here, :].astype(jnp.float32) + gate_ref[...] * total_ref[...]
+        gate = mod_ref[2, pl.ds(level_ref[0], 1), pl.ds(pl.multiple_of(t * width, width), width)]
+        updated = x_ref[here, :].astype(jnp.float32) + gate * total_ref[...]
         o_ref[here, :] = updated.astype(jnp.bfloat16)
         for e in range(1, shards):
             pl.when(t + e < shards)(lambda: right(c, t + e, right_ref).wait_send())
@@ -349,7 +369,7 @@
     lax.fori_loop(0, parts, finish, 0)
 
 
-def attend_project(live, queries, pieces, wo, x, gate):
+def attend_project(level, counts, mask, order, queries, pieces, wo, x, mod):
     sources, parts, _, heads, rows, _ = pieces.shape
     shards, width = lax.axis_size("tensor"), x.shape[1]
     vmem = pl.BlockSpec(memory_space=pltpu.VMEM)
@@ -358,7 +378,7 @@
     keys = sources * parts * rows
     return pl.pallas_call(
         attend_kernel,
-        in_specs=[pl.BlockSpec(memory_space=pltpu.SMEM), vmem, hbm, hbm, vmem, vmem],
+        in_specs=[pl.BlockSpec(memory_space=pltpu.SMEM)] * 4 + [vmem, hbm, hbm, vmem, vmem],
         out_specs=vmem,
         out_shape=jax.ShapeDtypeStruct(x.shape, jnp.bfloat16),
         scratch_shapes=[
@@ -375,7 +395,7 @@
             bytes_accessed=4 * keys * heads * HEAD_DIM,
             transcendentals=x.shape[0] * keys * heads,
         ),
-    )(live, queries, pieces, wo, x, gate)
+    )(level, counts, mask, order, queries, pieces, wo, x, mod)
 
 
 def on_device(
@@ -392,25 +412,13 @@
     block_mask,
     span_order,
 ):
-    shard_width = latents.shape[1]
-    spans = lax.axis_size("frame")
-    me = lax.axis_index("frame")
-    column_start = lax.axis_index("tensor") * shard_width
-    modulation = lax.dynamic_index_in_dim(mod_table, levels[0], 0, keepdims=False)
-    shift_row, scale_row, gate_row = modulation[0:1], modulation[1:2], modulation[2:3]
-
+    modulation = jnp.transpose(mod_table, (1, 0, 2))
     queries, pieces = gather_project(
-        latents, shift_row, scale_row, w_query, w_key, w_value, query_gain, key_gain, GATHER_PARTS
+        levels, latents, modulation, w_query, w_key, w_value, query_gain, key_gain, GATHER_PARTS
     )
-
-    offsets = jnp.arange(spans, dtype=jnp.int32)
-    span_of = lax.rem(jnp.where(offsets % 2 == 0, me, me ^ 1) + offsets // 2 * 2, spans)
-    own = offsets == 0
-    allowed = (span_order[span_of] <= span_order[me]) & ((block_mask[0][span_of] == 1) | own)
-    live = jnp.where(allowed, span_counts[span_of], 0).astype(jnp.int32)
-
-    gate_part = lax.dynamic_slice_in_dim(gate_row, column_start, shard_width, axis=1)
-    return attend_project(live, queries, pieces, w_out, latents, gate_part)
+    return attend_project(
+        levels, span_counts, block_mask, span_order, queries, pieces, w_out, latents, modulation
+    )
 
 
 def solution(mesh):

time: 248 us -> 236 us (0.952)
  local copies, waits for them, and re-layouts: 12.6 us -> 2.46 us
    gather x3 -> x0, local copies, waits for them, and re-layouts: 3.25 us -> none  [the longest x1 1.3 us: on_device(): span_order[span_of] <= span_order[me]]
    dynamic_slice x2 -> x0, local copies, waits for them, and re-layouts: 2.69 us -> none  [the longest x1 1.45 us: on_device(): lax.dynamic_slice_in_dim(gate_row, column_start, shard_width, axis=1)]
    broadcast_in_dim x2 -> x0, local copies, waits for them, and re-layouts: 2.57 us -> none  [the longest x1 1.28 us: gather_project(): qg[:, None, :]]
where the time goes in v4:
time: 236 us
  Pallas kernels  233 us (99%)
  local copies, waits for them, and re-layouts  2.46 us (1%)
    pallas_call x1, Pallas kernels, gather_project(): pl.pallas_call(gather_kernel, in_specs=[pl.BlockSpec(memory_space=pltpu.S...  121 us
    pallas_call x1, Pallas kernels, attend_project(): pl.pallas_call(attend_kernel, in_specs=[pl.BlockSpec(memory_space=pltpu.S...  111 us

profile of v4, /device:TPU:0, one launch (start us, length us, event | category | flops | bytes accessed | tf_op | source)
XLA Modules:
  0.0 235.8 jit_solution(15041286123019021165)
XLA Ops:
  0.7 121.5 %shard_map.118 = (bf16[4,6,128,128]{3,2,1,0:T(8,128)(2,1)}, bf16[8,4,2,6,128,128]{5,4,3,2,1,0:T(8,128)(2,1)}) custom-call(s32[1]{0:T(128)S(6)} %copy.14.level_ref, bf16[512,1280]{1,0:T(8,128)(2,1)} %x_ref.3, f32[3,16,5120]{2,1,0:T(8,128)} %bitcast.1, bf16[5120,768]{1,0:T(8,128)(2,1)} %wq_hbm.1, bf16[5120,768]{1,0:T(8,128)(2,1)} %wk_hbm.1, ...), custom_call_target="tpu_custom_call" | custom-call | flops 12079595520 | bytes 23592960 | tf_op jit(solution)/shard_map/pallas_call | solution.py:201
  122.1 111.2 %shard_map.119 = bf16[512,1280]{1,0:T(8,128)(2,1)} custom-call(s32[1]{0:T(128)S(6)} %copy.14.level_ref, s32[8]{0:T(128)} %counts_ref.1, s32[1,8]{1,0:T(1,128)} %mask_ref.1, s32[8]{0:T(128)} %order_ref.1, bf16[4,6,128,128]{3,2,1,0:T(8,128)(2,1)} %get-tuple-element.7.q_ref, bf16[8,4,2,6,128,128]{5,4,3,2,1,0:T(8,128)(2,1)} %get-tuple-element.8.kv_hbm, ...), custom_call_target="tpu_custom_call" | custom-call | flops 6442450944 | bytes 12582912 | tf_op jit(solution)/shard_map/pallas_call | solution.py:379
  233.3 2.5 %copy.15 = bf16[512,1280]{1,0:T(8,128)(2,1)} copy(bf16[512,1280]{1,0:T(8,128)(2,1)} %shard_map.119) | data formatting | bytes 2621440
